TPU v7x, 128 devices: a whole 4x4x4 slice. The times are simulated.
128 devices in a mesh: px: 8 (over z, core), py: 16 (over x, y).
Axes of the slice: x: 4, y: 4, z: 4, core: 2. Of those that a mesh axis runs over, the one named last changes fastest.
Arguments:
- coupling: bfloat16 [8, 16, 64, 218, 125], P('px', 'py'), may hold values from -0.5 to 0.5
- interior_inverse: bfloat16 [8, 16, 64, 125, 125], P('px', 'py'), may hold values from -0.5 to 0.5
- interior_load: bfloat16 [8, 16, 64, 125, 256], P('px', 'py'), may hold values from -6 to 6
- boundary_load: bfloat16 [8, 16, 4608, 256], P('px', 'py'), may hold values from -6 to 6
- owner_weight: float32 [8, 16, 4608], P('px', 'py'), may hold values from 0.5 to 4
- elem_weight: float32 [8, 16, 64, 218], P('px', 'py'), may hold values from 0.25 to 1
- elem_dof: int32 [8, 16, 64, 218], P('px', 'py'), may hold values from 0 to 5999, as said below
- reader_rows: int32 [8, 16, 4, 348], P('px', 'py'), may hold values from 0 to 4607, as said below
- elem_count: int32 [8, 16], P('px', 'py'), may hold values from 16 to 64, as said below
Outputs:
- face_values: float32 [8, 16, 4608, 256], P('px', 'py')
- interior_values: bfloat16 [8, 16, 64, 125, 256], P('px', 'py')
Inputs may be any that keep to these rules, and one draw needn't show every extreme that they name: `elem_dof`: rows below 4608 are the partition's own boundary rows; row 4608 + k * 348 + s is the s-th row that the partition shares with its neighbour in direction k. The modes of slot e name only rows r with r % 8 equal to e // 8. Every local row is named by at least two of the partition's modes. `reader_rows`: entry [k, s] is the owned row that the neighbour in direction k refers to by its row 4608 + opp(k) * 348 + s; the 1392 entries of one partition are distinct. `elem_count`: slots at or past a partition's count are empty.
All inputs are finite; a program needn't handle non-finite values.
Results may differ from a plain program's by a relative error of at most 0.0056.
Values may be sent and summed in bfloat16 or wider, within the bound.
No kernel may reach another device: no remote copies, remote signals or barrier semaphores. Data moves between devices by JAX's collectives and lax.ppermute only.
A program may use at most 128 MiB of HBM per device.

v0:
```python
import functools

import jax
import jax.numpy as jnp
from jax import lax
from jax.experimental import pallas as pl
from jax.experimental.pallas import tpu as pltpu
from jax.sharding import PartitionSpec as P

GS = 8
STEP = 16
LANES = 128
F32 = jnp.float32
BF16 = jnp.bfloat16


def up(value, multiple):
    return -(-value // multiple) * multiple


def passed_along(value, axis, steps):
    count = lax.axis_size(axis)
    pairs = [(source, (source + steps) % count) for source in range(count)]
    return lax.ppermute(value, axis, pairs)


def nn(a, b):
    return lax.dot_general(a, b, (((1,), (0,)), ((), ())), preferred_element_type=F32)


def tn(a, b):
    return lax.dot_general(a, b, (((0,), (0,)), ((), ())), preferred_element_type=F32)


def column_of(row):
    return jnp.transpose(jnp.broadcast_to(row, (LANES, LANES)))


def take(ref, at):
    parts = [ref[tile, at, :] for tile in range(ref.shape[0])]
    return parts[0] if len(parts) == 1 else jnp.concatenate(parts, axis=1)


def place(ref, at, rows):
    for tile in range(ref.shape[0]):
        ref[tile, at, :] = rows[:, tile * LANES : (tile + 1) * LANES]


def deinterleave(source, target):
    rows, slots, cols = source.shape
    for tile in range(target.shape[0]):
        first, end = tile * LANES, min((tile + 1) * LANES, cols)
        block = source[:, :, first:end].astype(F32).reshape(rows * slots, end - first)
        target[tile, 0 : rows * slots, 0 : end - first] = block


def slot_rows(target, slot, rows):
    return take(target, pl.ds(slot, rows, stride=STEP)).astype(BF16)


def clear(ref, first):
    if first < ref.shape[1]:
        ref[:, first:, :] = jnp.zeros((ref.shape[0], ref.shape[1] - first, ref.shape[2]), ref.dtype)


def condense_kernel(
    sizes,
    count_ref,
    readers_ref,
    dof_ref,
    weight_ref,
    owner_ref,
    edge_ref,
    load_ref,
    coupling_ref,
    inverse_ref,
    base_ref,
    pay0_ref,
    pay1_ref,
    pay2_ref,
    pay3_ref,
    load32,
    coup32,
    inv32,
    dofp,
    weightp,
    terms,
    onehot,
    wgroup,
    rows_nat,
    w_nat,
    picked,
):
    owned, shared, local, windows, modes, inner = sizes
    wpad = onehot.shape[0]
    step = pl.program_id(0)
    count = count_ref[0, 0]
    slots = dof_ref.shape[0]
    mpad = up(modes, 16)
    ipad = load32.shape[1] // STEP
    sp = up(shared, 16)

    @pl.when(step == 0)
    def _():
        clear(load32, inner * STEP)
        coup32[...] = jnp.zeros_like(coup32)
        inv32[...] = jnp.zeros_like(inv32)
        terms[...] = jnp.zeros_like(terms)
        live = lax.broadcasted_iota(jnp.int32, (slots, modes), 0) < count
        dofp[...] = jnp.full(dofp.shape, -1, jnp.int32)
        dofp[:, 0:modes] = jnp.where(live, lax.shift_right_arithmetic(dof_ref[...], 3), -1)
        weightp[...] = jnp.zeros_like(weightp)
        weightp[:, 0:modes] = weight_ref[...]
        clear(rows_nat, local)
        w_nat[local:, :] = jnp.zeros((w_nat.shape[0] - local, w_nat.shape[1]), F32)
        for k in range(4):
            picked[:, k * sp + shared : (k + 1) * sp, :] = jnp.zeros((3, sp - shared, LANES), F32)

    deinterleave(load_ref, load32)
    deinterleave(coupling_ref, coup32)
    deinterleave(inverse_ref, inv32)

    for half in range(STEP // GS):
        group = step * (STEP // GS) + half
        for e in range(GS):
            slot = half * GS + e
            solved = nn(slot_rows(inv32, slot, ipad), slot_rows(load32, slot, ipad)).astype(BF16)
            term = nn(slot_rows(coup32, slot, mpad), solved)
            terms[e * 256 : e * 256 + mpad, :] = term.astype(BF16)

        dofs = dofp[pl.ds(pl.multiple_of(group * GS, GS), GS), :]
        weights = weightp[pl.ds(pl.multiple_of(group * GS, GS), GS), :]

        def fill(chunk, _):
            ids = lax.broadcasted_iota(jnp.int32, (16, 256), 0) + chunk * 16
            total = jnp.zeros((16, 256), F32)
            for e in range(GS):
                hit = ids == jnp.broadcast_to(dofs[e : e + 1], (16, 256))
                onehot[pl.ds(pl.multiple_of(chunk * 16, 16), 16), e * 256 : (e + 1) * 256] = jnp.where(
                    hit, 1.0, 0.0
                ).astype(BF16)
                total = total + jnp.where(hit, jnp.broadcast_to(weights[e : e + 1], (16, 256)), 0.0)
            wgroup[pl.ds(pl.multiple_of(chunk * 16, 16), 16), :] = jnp.broadcast_to(
                jnp.sum(total, axis=1, keepdims=True), (16, LANES)
            )
            return 0

        lax.fori_loop(0, wpad // 16, fill, 0)
        place(rows_nat, pl.ds(group, windows, stride=GS), nn(onehot[...], terms[...])[0:windows])
        w_nat[pl.ds(group, windows, stride=GS), :] = wgroup[0:windows, :]

    @pl.when(step == pl.num_programs(0) - 1)
    def _():
        def finish(q, _):
            at = pl.ds(pl.multiple_of(q * LANES, LANES), LANES)
            weight = w_nat[at, :] + column_of(owner_ref[pl.ds(q, 1), :])
            w_nat[at, :] = weight
            total = edge_ref[at, :].astype(F32) - take(rows_nat, at)
            place(rows_nat, at, total)
            inv_weight = 1.0 / weight
            base_ref[at, :] = total * jnp.concatenate([inv_weight, inv_weight], axis=1)
            return 0

        lax.fori_loop(0, owned // LANES, finish, 0)

        batch = 12
        for k in range(4):

            def pick(i, _):
                for j in range(batch):
                    s = i * batch + j
                    row = readers_ref[k, s]
                    picked[0, pl.ds(k * sp + s, 1), :] = rows_nat[0, pl.ds(row, 1), :]
                    picked[1, pl.ds(k * sp + s, 1), :] = rows_nat[1, pl.ds(row, 1), :]
                    picked[2, pl.ds(k * sp + s, 1), :] = w_nat[pl.ds(row, 1), :]
                return 0

            lax.fori_loop(0, shared // batch, pick, 0)

        low = lax.broadcasted_iota(jnp.int32, (sp, LANES), 1) < LANES // 2

        def packed(weight):
            high = weight.astype(BF16).astype(F32)
            return jnp.where(low, high, weight - high).astype(BF16)

        for k, pay in enumerate((pay0_ref, pay1_ref, pay2_ref, pay3_ref)):
            first = owned + k * shared
            for tile in range(2):
                lane = slice(tile * LANES, (tile + 1) * LANES)
                pay[0:sp, lane] = rows_nat[tile, first : first + sp, :].astype(BF16)
                pay[sp : 2 * sp, lane] = picked[tile, k * sp : (k + 1) * sp, :].astype(BF16)
            pay[0:sp, 256:384] = packed(w_nat[first : first + sp, :])
            pay[sp : 2 * sp, 256:384] = packed(picked[2, k * sp : (k + 1) * sp, :])


def recover_kernel(
    sizes,
    count_ref,
    readers_ref,
    dof_ref,
    base_ref,
    pay0_ref,
    pay1_ref,
    pay2_ref,
    pay3_ref,
    in0_ref,
    in1_ref,
    in2_ref,
    in3_ref,
    load_ref,
    coupling_ref,
    inverse_ref,
    face_ref,
    out_ref,
    load32,
    coup32,
    inv32,
    out32,
    dofp,
    onehot,
    window,
    boundary,
    values,
    shares,
    in_sem,
    out_sem,
):
    owned, shared, local, windows, modes, inner = sizes
    step = pl.program_id(0)
    last = pl.num_programs(0) - 1
    count = count_ref[0, 0]
    slots = dof_ref.shape[0]
    mpad = up(modes, 16)
    ipad = load32.shape[1] // STEP
    sp = up(shared, 16)
    wpad = window.shape[0]

    def copies(out):
        pairs = []
        for tile in range(2):
            here = values.at[tile, pl.ds(0, owned)]
            lane = pl.ds(tile * LANES, LANES)
            if out:
                pairs.append(pltpu.make_async_copy(here, face_ref.at[:, lane], out_sem.at[tile]))
            else:
                pairs.append(pltpu.make_async_copy(base_ref.at[:, lane], here, in_sem.at[tile]))
        return pairs

    @pl.when(step == 0)
    def _():
        for copy in copies(False):
            copy.start()
        clear(load32, inner * STEP)
        coup32[...] = jnp.zeros_like(coup32)
        inv32[...] = jnp.zeros_like(inv32)
        dofp[...] = jnp.full(dofp.shape, -1, jnp.int32)
        dofp[:, 0:modes] = lax.shift_right_arithmetic(dof_ref[...], 3)
        clear(values, local)
        window[...] = jnp.zeros_like(window)

        def quotient(total, theirs, mine):
            weight = theirs.astype(F32) + mine.astype(F32)
            inverse = 1.0 / (weight + pltpu.roll(weight, LANES // 2, 1))
            return total * jnp.concatenate([inverse, inverse], axis=1)

        pays = (pay0_ref, pay1_ref, pay2_ref, pay3_ref)
        arrived = (in0_ref, in1_ref, in2_ref, in3_ref)
        for k in range(4):
            pay, inc = pays[k], arrived[k]
            mine = quotient(
                pay[sp : 2 * sp, 0:256].astype(F32) - inc[0:sp, 0:256].astype(F32),
                pay[sp : 2 * sp, 256:384],
                inc[0:sp, 256:384],
            )
            place(shares, slice(k * sp, (k + 1) * sp), mine)
            first = owned + k * shared
            theirs = quotient(
                inc[sp : 2 * sp, 0:256].astype(F32) - pay[0:sp, 0:256].astype(F32),
                inc[sp : 2 * sp, 256:384],
                pay[0:sp, 256:384],
            )
            place(values, slice(first, first + shared), theirs[0:shared])
        for copy in copies(False):
            copy.wait()
        batch = 12
        for k in range(4):

            def put(i, _):
                for j in range(batch):
                    s = i * batch + j
                    row = readers_ref[k, s]
                    for tile in range(2):
                        values[tile, pl.ds(row, 1), :] = shares[tile, pl.ds(k * sp + s, 1), :]
                return 0

            lax.fori_loop(0, shared // batch, put, 0)
        for copy in copies(True):
            copy.start()

    deinterleave(load_ref, load32)
    deinterleave(coupling_ref, coup32)
    deinterleave(inverse_ref, inv32)

    for half in range(STEP // GS):
        group = step * (STEP // GS) + half
        window[0:windows, :] = take(values, pl.ds(group, windows, stride=GS)).astype(BF16)
        dofs = dofp[pl.ds(pl.multiple_of(group * GS, GS), GS), :]
        lanes = lax.broadcasted_iota(jnp.int32, (LANES, wpad), 1)
        for e in range(GS):
            for part in range(2):
                rows = min(LANES, mpad - part * LANES)
                column = column_of(dofs[e : e + 1, part * LANES : (part + 1) * LANES])
                wide = jnp.concatenate([column] * (wpad // LANES), axis=1)
                hit = jnp.where(wide == lanes, 1.0, 0.0).astype(BF16)
                start = e * mpad + part * LANES
                onehot[start : start + rows, :] = hit[0:rows]
        boundary[...] = nn(onehot[...], window[...]).astype(BF16)
        for e in range(GS):
            slot = half * GS + e
            pulled = tn(slot_rows(coup32, slot, mpad), boundary[e * mpad : (e + 1) * mpad, :])
            reduced = (take(load32, pl.ds(slot, ipad, stride=STEP)) - pulled).astype(BF16)
            result = nn(slot_rows(inv32, slot, ipad), reduced)
            result = jnp.where(group * GS + e < count, result, 0.0)
            place(out32, pl.ds(slot, ipad, stride=STEP), result)

    for tile in range(2):
        block = out32[tile, 0 : inner * STEP, :].reshape(inner, STEP, LANES)
        out_ref[:, :, tile * LANES : (tile + 1) * LANES] = block.astype(BF16)

    @pl.when(step == last)
    def _():
        for copy in copies(True):
            copy.wait()


def whole(shape):
    zeros = (0,) * len(shape)
    return pl.BlockSpec(shape, lambda step: zeros)


def by_slot(rows, cols):
    return pl.BlockSpec((rows, STEP, cols), lambda step: (0, step, 0))


def per_device(
    coupling,
    interior_inverse,
    interior_load,
    boundary_load,
    owner_weight,
    elem_weight,
    elem_dof,
    reader_rows,
    elem_count,
):
    coupling = jnp.transpose(coupling[0, 0], (1, 0, 2))
    inverse = jnp.transpose(interior_inverse[0, 0], (1, 0, 2))
    load = jnp.transpose(interior_load[0, 0], (1, 0, 2))
    edge_load = boundary_load[0, 0]
    owner = owner_weight[0, 0].reshape(-1, LANES)
    weight = elem_weight[0, 0]
    dof = elem_dof[0, 0]
    readers = reader_rows[0, 0]

    modes, slots, inner = coupling.shape
    columns = load.shape[-1]
    owned = edge_load.shape[0]
    shared = readers.shape[1]
    local = owned + 4 * shared
    windows = local // GS
    sp = up(shared, 16)
    mpad = up(modes, 16)
    ipad = up(inner, 16)
    nat = up(local + sp - shared, 16)
    sizes = (owned, shared, local, windows, modes, inner)
    steps = slots // STEP
    smem = pl.BlockSpec(memory_space=pltpu.SMEM)
    anywhere = pl.BlockSpec(memory_space=pl.ANY)
    params = pltpu.CompilerParams(
        vmem_limit_bytes=60 * 2**20, dimension_semantics=("arbitrary",)
    )
    pay_shape = jax.ShapeDtypeStruct((2 * sp, 384), BF16)
    work = [
        pltpu.VMEM((2, ipad * STEP, LANES), F32),
        pltpu.VMEM((1, mpad * STEP, LANES), F32),
        pltpu.VMEM((1, ipad * STEP, LANES), F32),
    ]
    big = [by_slot(inner, columns), by_slot(modes, inner), by_slot(inner, inner)]

    base, *pays = pl.pallas_call(
        functools.partial(condense_kernel, sizes),
        grid=(steps,),
        in_specs=[smem, smem, whole(dof.shape), whole(weight.shape), whole(owner.shape), whole(edge_load.shape)]
        + big,
        out_specs=[whole((owned, columns))] + [whole(pay_shape.shape)] * 4,
        out_shape=[jax.ShapeDtypeStruct((owned, columns), F32)] + [pay_shape] * 4,
        scratch_shapes=work
        + [
            pltpu.VMEM((slots, 256), jnp.int32),
            pltpu.VMEM((slots, 256), F32),
            pltpu.VMEM((GS * 256, columns), BF16),
            pltpu.VMEM((up(windows, 16), GS * 256), BF16),
            pltpu.VMEM((up(windows, 16), LANES), F32),
            pltpu.VMEM((2, nat, LANES), F32),
            pltpu.VMEM((nat, LANES), F32),
            pltpu.VMEM((3, 4 * sp, LANES), F32),
        ],
        compiler_params=params,
        name="condense",
    )(elem_count, readers, dof, weight, owner, edge_load, load, coupling, inverse)

    arrived = [
        passed_along(pays[1], "px", 1),
        passed_along(pays[0], "px", -1),
        passed_along(pays[3], "py", 1),
        passed_along(pays[2], "py", -1),
    ]

    face, interior = pl.pallas_call(
        functools.partial(recover_kernel, sizes),
        grid=(steps,),
        in_specs=[smem, smem, whole(dof.shape), anywhere] + [whole(pay_shape.shape)] * 8 + big,
        out_specs=[anywhere, by_slot(inner, columns)],
        out_shape=[
            jax.ShapeDtypeStruct((owned, columns), F32),
            jax.ShapeDtypeStruct((inner, slots, columns), BF16),
        ],
        scratch_shapes=work
        + [
            pltpu.VMEM((2, ipad * STEP, LANES), F32),
            pltpu.VMEM((slots, 256), jnp.int32),
            pltpu.VMEM((GS * mpad, up(windows, LANES)), BF16),
            pltpu.VMEM((up(windows, LANES), columns), BF16),
            pltpu.VMEM((GS * mpad, columns), BF16),
            pltpu.VMEM((2, nat, LANES), F32),
            pltpu.VMEM((2, 4 * sp, LANES), F32),
            pltpu.SemaphoreType.DMA((2,)),
            pltpu.SemaphoreType.DMA((2,)),
        ],
        compiler_params=params,
        name="recover",
    )(elem_count, readers, dof, base, *pays, *arrived, load, coupling, inverse)
    interior = jnp.transpose(interior, (1, 0, 2))
    return (face[None, None], interior[None, None])


def solution(mesh):
    in_specs = (
        P("px", "py", None, None, None),
        P("px", "py", None, None, None),
        P("px", "py", None, None, None),
        P("px", "py", None, None),
        P("px", "py", None),
        P("px", "py", None, None),
        P("px", "py", None, None),
        P("px", "py", None, None),
        P("px", "py"),
    )
    out_specs = (P("px", "py", None, None), P("px", "py", None, None, None))
    return jax.shard_map(
        per_device, mesh=mesh, in_specs=in_specs, out_specs=out_specs, check_vma=False
    )
```

profile of v0, /device:TPU:1, one launch (start us, length us, event | category | flops | bytes accessed | tf_op | source)
XLA Modules:
  0.0 136.3 jit_solution(1525598619494456374)
XLA Ops:
  1.3 1.4 %reduce = f32[4608]{0:T(1024)} reduce(f32[1,1,4608]{2,1,0:T(1,128)} %param.13, f32[]{:T(128)} %constant.9), dimensions={0,1}, to_apply=%param.13.reduce_sub_computation | reduce | bytes 36868 | tf_op args[4]
  2.7 72.6 %condense.1 = (f32[4608,256]{1,0:T(8,128)}, bf16[704,384]{1,0:T(8,128)(2,1)}, bf16[704,384]{1,0:T(8,128)(2,1)}, bf16[704,384]{1,0:T(8,128)(2,1)}, bf16[704,384]{1,0:T(8,128)(2,1)}) custom-call(s32[1,1]{1,0:T(1,128)S(6)} %copy.11.count_ref, s32[4,348]{1,0:T(4,128)} %bitcast.29, s32[64,218]{1,0:T(8,128)} %bitcast.25, f32[64,218]{1,0:T(8,128)} %bitcast.28, ...), custom_call_target="tpu_custom_call" | custom-call | tf_op jit(solution)/shard_map/condense/pallas_call | solution.py:390
  75.3 1.4 %collective-permute-start.1 = (bf16[704,384]{1,0:T(8,128)(2,1)}, bf16[704,384]{1,0:T(8,128)(2,1)S(1)}, u32[]{:S(2)}, u32[]{:S(2)}) collective-permute-start(bf16[704,384]{1,0:T(8,128)(2,1)} %get-tuple-element.10.pay0_ref), channel_id=1, source_target_pairs={{0,112},{16,0},{32,16},{48,32},{64,48},{80,64},{96,80},{112,96},{1... | collective-permute-start | bytes 1622024 | tf_op jit(solution)/shard_map/ppermute | solution.py:24
  76.7 1.6 %collective-permute-start = (bf16[704,384]{1,0:T(8,128)(2,1)}, bf16[704,384]{1,0:T(8,128)(2,1)S(1)}, u32[]{:S(2)}, u32[]{:S(2)}) collective-permute-start(bf16[704,384]{1,0:T(8,128)(2,1)} %get-tuple-element.11.pay1_ref), channel_id=1, source_target_pairs={{0,16},{16,32},{32,48},{48,64},{64,80},{80,96},{96,112},{112,0},{1... | collective-permute-start | bytes 1622024 | tf_op jit(solution)/shard_map/ppermute | solution.py:24
  78.3 4.9 %collective-permute-start.3 = (bf16[704,384]{1,0:T(8,128)(2,1)}, bf16[704,384]{1,0:T(8,128)(2,1)S(1)}, u32[]{:S(2)}, u32[]{:S(2)}) collective-permute-start(bf16[704,384]{1,0:T(8,128)(2,1)} %get-tuple-element.12.pay2_ref), channel_id=1, source_target_pairs={{0,15},{1,0},{2,1},{3,2},{4,3},{5,4},{6,5},{7,6},{8,7},{9,8},{10,9... | collective-permute-start | bytes 1622024 | tf_op jit(solution)/shard_map/ppermute | solution.py:24
  83.3 0.0 collective-permute-start.2
  83.3 2.6 %collective-permute-done.1.in1_ref = bf16[704,384]{1,0:T(8,128)(2,1)S(1)} collective-permute-done((bf16[704,384]{1,0:T(8,128)(2,1)}, bf16[704,384]{1,0:T(8,128)(2,1)S(1)}, u32[]{:S(2)}, u32[]{:S(2)}) %collective-permute-start.1) | collective-permute-done | bytes 540704 | tf_op jit(solution)/shard_map/ppermute | solution.py:24
  85.9 0.0 copy-start
  85.9 0.0 collective-permute-done.in0_ref
  85.9 0.0 copy-start.1
  85.9 7.3 %collective-permute-done.3.in3_ref = bf16[704,384]{1,0:T(8,128)(2,1)S(1)} collective-permute-done((bf16[704,384]{1,0:T(8,128)(2,1)}, bf16[704,384]{1,0:T(8,128)(2,1)S(1)}, u32[]{:S(2)}, u32[]{:S(2)}) %collective-permute-start.3) | collective-permute-done | bytes 540704 | tf_op jit(solution)/shard_map/ppermute | solution.py:24
  93.2 0.0 copy-start.2
  93.2 5.1 %collective-permute-done.2.in2_ref = bf16[704,384]{1,0:T(8,128)(2,1)S(1)} collective-permute-done((bf16[704,384]{1,0:T(8,128)(2,1)}, bf16[704,384]{1,0:T(8,128)(2,1)S(1)}, u32[]{:S(2)}, u32[]{:S(2)}) %collective-permute-start.2) | collective-permute-done | bytes 540704 | tf_op jit(solution)/shard_map/ppermute | solution.py:24
  98.3 0.0 copy-start.3
  98.3 0.0 copy-done
  98.3 0.0 copy-done.1
  98.3 0.0 copy-done.2
  98.4 0.8 copy-done.3
  99.2 37.0 %recover.1 = (f32[4608,256]{1,0:T(8,128)}, bf16[125,64,256]{2,1,0:T(8,128)(2,1)}) custom-call(s32[1,1]{1,0:T(1,128)S(6)} %copy.11.count_ref, s32[4,348]{1,0:T(4,128)} %bitcast.30, s32[64,218]{1,0:T(8,128)} %bitcast.26, f32[4608,256]{1,0:T(8,128)} %get-tuple-element.9.base_ref, bf16[704,384]{1,0:T(8,128)(2,1)} %get-tuple-element.10.pay0_ref, ...), custom_call_target="tpu_custom_call" | custom-call | tf_op jit(solution)/shard_map/recover/pallas_call | solution.py:419
Async XLA Ops:
  75.3 10.6 %collective-permute-start.1 = (bf16[704,384]{1,0:T(8,128)(2,1)}, bf16[704,384]{1,0:T(8,128)(2,1)S(1)}, u32[]{:S(2)}, u32[]{:S(2)}) collective-permute-start(bf16[704,384]{1,0:T(8,128)(2,1)} %get-tuple-element.10.pay0_ref), channel_id=1, source_target_pairs={{0,112},{16,0},{32,16},{48,32},{64,48},{80,64},{96,80},{112,96},{1... | collective-permute-start | bytes 1622024 | tf_op jit(solution)/shard_map/ppermute | solution.py:24
  76.7 9.2 %collective-permute-start = (bf16[704,384]{1,0:T(8,128)(2,1)}, bf16[704,384]{1,0:T(8,128)(2,1)S(1)}, u32[]{:S(2)}, u32[]{:S(2)}) collective-permute-start(bf16[704,384]{1,0:T(8,128)(2,1)} %get-tuple-element.11.pay1_ref), channel_id=1, source_target_pairs={{0,16},{16,32},{32,48},{48,64},{64,80},{80,96},{96,112},{112,0},{1... | collective-permute-start | bytes 1622024 | tf_op jit(solution)/shard_map/ppermute | solution.py:24
  78.3 14.9 %collective-permute-start.3 = (bf16[704,384]{1,0:T(8,128)(2,1)}, bf16[704,384]{1,0:T(8,128)(2,1)S(1)}, u32[]{:S(2)}, u32[]{:S(2)}) collective-permute-start(bf16[704,384]{1,0:T(8,128)(2,1)} %get-tuple-element.12.pay2_ref), channel_id=1, source_target_pairs={{0,15},{1,0},{2,1},{3,2},{4,3},{5,4},{6,5},{7,6},{8,7},{9,8},{10,9... | collective-permute-start | bytes 1622024 | tf_op jit(solution)/shard_map/ppermute | solution.py:24
  83.3 15.1 %collective-permute-start.2 = (bf16[704,384]{1,0:T(8,128)(2,1)}, bf16[704,384]{1,0:T(8,128)(2,1)S(1)}, u32[]{:S(2)}, u32[]{:S(2)}) collective-permute-start(bf16[704,384]{1,0:T(8,128)(2,1)} %get-tuple-element.13.pay3_ref), channel_id=1, source_target_pairs={{0,1},{1,2},{2,3},{3,4},{4,5},{5,6},{6,7},{7,8},{8,9},{9,10},{10,1... | collective-permute-start | bytes 1622024 | tf_op jit(solution)/shard_map/ppermute | solution.py:24
  85.9 12.5 %copy-start = (bf16[704,384]{1,0:T(8,128)(2,1)}, bf16[704,384]{1,0:T(8,128)(2,1)S(1)}, u32[]{:S(2)}) copy-start(bf16[704,384]{1,0:T(8,128)(2,1)S(1)} %collective-permute-done.1.in1_ref) | copy-start | bytes 1622020
  85.9 12.5 %copy-start.1 = (bf16[704,384]{1,0:T(8,128)(2,1)}, bf16[704,384]{1,0:T(8,128)(2,1)S(1)}, u32[]{:S(2)}) copy-start(bf16[704,384]{1,0:T(8,128)(2,1)S(1)} %collective-permute-done.in0_ref) | copy-start | bytes 1622020
  93.2 5.1 %copy-start.2 = (bf16[704,384]{1,0:T(8,128)(2,1)}, bf16[704,384]{1,0:T(8,128)(2,1)S(1)}, u32[]{:S(2)}) copy-start(bf16[704,384]{1,0:T(8,128)(2,1)S(1)} %collective-permute-done.3.in3_ref) | copy-start | bytes 1622020
  98.3 0.8 copy-start.3
where the time goes:
time: 138 us; the launch traced here: 136 us
  Pallas kernels  110 us (80%)
  waiting for transfers between devices  15.1 us (11%)
  starting transfers between devices  7.98 us (6%)
  between operations  1.45 us (1%)
    pallas_call x1, Pallas kernels, per_device(): pl.pallas_call(functools.partial(condense_kernel, sizes), grid=(steps,),...  72.6 us
    pallas_call x1, Pallas kernels, per_device(): pl.pallas_call(functools.partial(recover_kernel, sizes), grid=(steps,), i...  37 us
    ppermute x4, waiting for transfers between devices, passed_along(): return lax.ppermute(value, axis, pairs)  15.1 us
    ppermute x4, starting transfers between devices, passed_along(): return lax.ppermute(value, axis, pairs)  7.98 us
  transfers between devices with their start and end apart: 4, of which 3 were waited for; matrix products, arithmetic and copies ran while one was open for 0% of the time, Pallas kernels for 0%

commit v1 on v0

v1 whole, which is shorter than its diff:
```python
import functools

import jax
import jax.numpy as jnp
from jax import lax
from jax.experimental import pallas as pl
from jax.experimental.pallas import tpu as pltpu
from jax.sharding import PartitionSpec as P

GS = 8
STEP = 16
LANES = 128
F32 = jnp.float32
BF16 = jnp.bfloat16


def up(value, multiple):
    return -(-value // multiple) * multiple


def passed_along(value, axis, steps):
    count = lax.axis_size(axis)
    pairs = [(source, (source + steps) % count) for source in range(count)]
    return lax.ppermute(value, axis, pairs)


def nn(a, b):
    return lax.dot_general(a, b, (((1,), (0,)), ((), ())), preferred_element_type=F32)


def tn(a, b):
    return lax.dot_general(a, b, (((0,), (0,)), ((), ())), preferred_element_type=F32)


def column_of(row):
    return jnp.transpose(jnp.broadcast_to(row, (LANES, LANES)))


def take(ref, at):
    parts = [ref[tile, at, :] for tile in range(ref.shape[0])]
    return parts[0] if len(parts) == 1 else jnp.concatenate(parts, axis=1)


def place(ref, at, rows):
    for tile in range(ref.shape[0]):
        ref[tile, at, :] = rows[:, tile * LANES : (tile + 1) * LANES]


def deinterleave(source, target):
    rows, slots, cols = source.shape
    for tile in range(target.shape[0]):
        first, end = tile * LANES, min((tile + 1) * LANES, cols)
        block = source[:, :, first:end].astype(F32).reshape(rows * slots, end - first)
        target[tile, 0 : rows * slots, 0 : end - first] = block


def slot_rows(target, slot, rows):
    return take(target, pl.ds(slot, rows, stride=STEP)).astype(BF16)


def clear(ref, first):
    if first < ref.shape[1]:
        ref[:, first:, :] = jnp.zeros((ref.shape[0], ref.shape[1] - first, ref.shape[2]), ref.dtype)


def solve_kernel(
    sizes,
    count_ref,
    dof_ref,
    weight_ref,
    load_ref,
    coupling_ref,
    inverse_ref,
    pairs_ref,
    coup_ref,
    solved_ref,
    high_ref,
    head_ref,
    headw_ref,
    pay0_ref,
    pay1_ref,
    pay2_ref,
    pay3_ref,
    dofp,
    weightp,
    load32,
    coup32,
    inv32,
    rows_nat,
    w_nat,
):
    owned, shared, local, windows, modes, inner, cut = sizes
    step = pl.program_id(0)
    mpad, ipad, sp = up(modes, 16), up(inner, LANES), up(shared, 16)

    @pl.when(step == 0)
    def _():
        clear(load32, inner * STEP)
        coup32[...] = jnp.zeros_like(coup32)
        inv32[...] = jnp.zeros_like(inv32)
        live = lax.broadcasted_iota(jnp.int32, dof_ref.shape, 0) < count_ref[0, 0]
        dofp[...] = jnp.full(dofp.shape, -1, jnp.int32)
        dofp[:, 0:modes] = jnp.where(live, lax.shift_right_arithmetic(dof_ref[...], 3), -1)
        weightp[...] = jnp.zeros_like(weightp)
        weightp[:, 0:modes] = weight_ref[...]

    deinterleave(load_ref, load32)
    deinterleave(coupling_ref, coup32)
    deinterleave(inverse_ref, inv32)

    zeros = jnp.zeros((ipad, LANES), BF16)
    for half in range(STEP // GS):
        group = step * (STEP // GS) + half
        at = pl.ds(pl.multiple_of(group * GS, GS), GS)
        for p in range(GS // 2):
            slot = half * GS + 2 * p
            pair = slot // 2
            pairs_ref[pair, 0:ipad, 0:LANES] = slot_rows(inv32, slot, ipad)
            pairs_ref[pair, 0:ipad, LANES:] = zeros
            pairs_ref[pair, ipad:, 0:LANES] = zeros
            pairs_ref[pair, ipad:, LANES:] = slot_rows(inv32, slot + 1, ipad)
            loads = jnp.concatenate(
                [slot_rows(load32, slot, ipad), slot_rows(load32, slot + 1, ipad)], axis=0
            )
            solved_ref[half, 2 * p * ipad : (2 * p + 2) * ipad, :] = nn(pairs_ref[pair], loads).astype(BF16)
        for e in range(GS):
            slot = half * GS + e
            coup_ref[slot] = slot_rows(coup32, slot, mpad)
        totals = operator(
            dofp[at, :],
            weightp[at, :],
            lambda e: coup_ref[half * GS + e],
            high_ref.at[half],
            cut,
            mpad,
        )
        place(rows_nat, pl.ds(group, high_ref.shape[1], stride=GS), nn(high_ref[half], solved_ref[half]))
        w_nat[pl.ds(group, high_ref.shape[1], stride=GS), :] = totals

    @pl.when(step == pl.num_programs(0) - 1)
    def _():
        begin = owned - cut * GS
        for tile in range(2):
            head_ref[tile] = rows_nat[tile, 0:begin, :]
        headw_ref[...] = w_nat[0:begin, :]
        low = lax.broadcasted_iota(jnp.int32, (sp, LANES), 1) < LANES // 2
        for k, pay in enumerate((pay0_ref, pay1_ref, pay2_ref, pay3_ref)):
            first = begin + k * shared
            for tile in range(2):
                lane = slice(tile * LANES, (tile + 1) * LANES)
                pay[:, lane] = rows_nat[tile, first : first + sp, :].astype(BF16)
            weight = w_nat[first : first + sp, :]
            top = weight.astype(BF16).astype(F32)
            pay[:, 256:384] = jnp.where(low, top, weight - top).astype(BF16)


def operator(dofs, weights, coupling_of, target, first, mpad):
    count = target.shape[0]
    block = 16
    parts = []
    for chunk in range(0, count, block):
        ids = lax.broadcasted_iota(jnp.int32, (block, 256), 0) + (first + chunk)
        total = jnp.zeros((block, 256), F32)
        for e in range(GS):
            hit = ids == jnp.broadcast_to(dofs[e : e + 1], (block, 256))
            total = total + jnp.where(hit, jnp.broadcast_to(weights[e : e + 1], (block, 256)), 0.0)
        parts.append(total)
    ids = lax.broadcasted_iota(jnp.int32, (count, 256), 0) + first
    for e in range(GS):
        hit = jnp.where(ids == jnp.broadcast_to(dofs[e : e + 1], (count, 256)), 1.0, 0.0).astype(BF16)
        target[:, e * LANES : (e + 1) * LANES] = nn(hit[:, 0:mpad], coupling_of(e)).astype(BF16)
    total = jnp.concatenate(parts, axis=0)
    return jnp.broadcast_to(jnp.sum(total, axis=1, keepdims=True), (count, LANES))


def owned_kernel(
    sizes,
    count_ref,
    readers_ref,
    dof_ref,
    weight_ref,
    owner_ref,
    edge_ref,
    head_ref,
    headw_ref,
    coup_ref,
    solved_ref,
    low_ref,
    total_ref,
    totalw_ref,
    picked_ref,
    dofp,
    weightp,
):
    owned, shared, local, windows, modes, inner, cut = sizes
    step = pl.program_id(0)
    mpad, sp = up(modes, 16), up(shared, 16)

    @pl.when(step == 0)
    def _():
        live = lax.broadcasted_iota(jnp.int32, dof_ref.shape, 0) < count_ref[0, 0]
        dofp[...] = jnp.full(dofp.shape, -1, jnp.int32)
        dofp[:, 0:modes] = jnp.where(live, lax.shift_right_arithmetic(dof_ref[...], 3), -1)
        weightp[...] = jnp.zeros_like(weightp)
        weightp[:, 0:modes] = weight_ref[...]
        for q in range(owned // LANES):
            totalw_ref[q * LANES : (q + 1) * LANES, :] = column_of(owner_ref[q : q + 1, :])
        for tile in range(2):
            total_ref[tile] = edge_ref[:, tile * LANES : (tile + 1) * LANES].astype(F32)
            total_ref[tile, cut * GS :, :] -= head_ref[tile]
            picked_ref[tile] = jnp.zeros(picked_ref.shape[1:], F32)
        totalw_ref[cut * GS :, :] += headw_ref[...]
        picked_ref[2] = jnp.ones(picked_ref.shape[1:], F32)

    for half in range(STEP // GS):
        group = step * (STEP // GS) + half
        at = pl.ds(pl.multiple_of(group * GS, GS), GS)
        totals = operator(
            dofp[at, :],
            weightp[at, :],
            lambda e: coup_ref[half * GS + e],
            low_ref.at[half],
            0,
            mpad,
        )
        rows = pl.ds(group, cut, stride=GS)
        place(total_ref, rows, take(total_ref, rows) - nn(low_ref[half], solved_ref[half]))
        totalw_ref[rows, :] = totalw_ref[rows, :] + totals

    @pl.when(step == pl.num_programs(0) - 1)
    def _():
        batch = 12
        for k in range(4):

            def pick(i, _):
                for j in range(batch):
                    s = i * batch + j
                    row = readers_ref[k, s]
                    picked_ref[0, pl.ds(k * sp + s, 1), :] = total_ref[0, pl.ds(row, 1), :]
                    picked_ref[1, pl.ds(k * sp + s, 1), :] = total_ref[1, pl.ds(row, 1), :]
                    picked_ref[2, pl.ds(k * sp + s, 1), :] = totalw_ref[pl.ds(row, 1), :]
                return 0

            lax.fori_loop(0, shared // batch, pick, 0)


def shares_kernel(picked_ref, in0_ref, in1_ref, in2_ref, in3_ref, shares_ref, send0_ref, send1_ref, send2_ref, send3_ref):
    arrived = (in0_ref, in1_ref, in2_ref, in3_ref)
    sends = (send0_ref, send1_ref, send2_ref, send3_ref)
    sp = in0_ref.shape[0]
    for k in range(4):
        at = slice(k * sp, (k + 1) * sp)
        weight = arrived[k][:, 256:384].astype(F32)
        inverse = 1.0 / (picked_ref[2, at, :] + weight + pltpu.roll(weight, LANES // 2, 1))
        for tile in range(2):
            lane = slice(tile * LANES, (tile + 1) * LANES)
            value = (picked_ref[tile, at, :] - arrived[k][:, lane].astype(F32)) * inverse
            shares_ref[tile, at, :] = value
            sends[k][:, lane] = value.astype(BF16)


def face_kernel(sizes, readers_ref, total_ref, totalw_ref, shares_ref, face_ref, window_ref, values):
    owned, shared, local, windows, modes, inner, cut = sizes
    sp = up(shared, 16)
    size = 512

    def divide(q, _):
        at = pl.ds(pl.multiple_of(q * size, size), size)
        inverse = 1.0 / totalw_ref[at, :]
        for tile in range(2):
            values[tile, at, :] = total_ref[tile, at, :] * inverse
        return 0

    lax.fori_loop(0, owned // size, divide, 0)
    batch = 12
    for k in range(4):

        def put(i, _):
            for j in range(batch):
                s = i * batch + j
                row = readers_ref[k, s]
                for tile in range(2):
                    values[tile, pl.ds(row, 1), :] = shares_ref[tile, pl.ds(k * sp + s, 1), :]
            return 0

        lax.fori_loop(0, shared // batch, put, 0)
    for tile in range(2):
        face_ref[:, tile * LANES : (tile + 1) * LANES] = values[tile]
    for group in range(GS):
        window_ref[group] = take(values, pl.ds(group, owned // GS, stride=GS)).astype(BF16)


def recover_kernel(
    sizes,
    count_ref,
    in0_ref,
    in1_ref,
    in2_ref,
    in3_ref,
    window_ref,
    low_ref,
    high_ref,
    load_ref,
    pairs_ref,
    out_ref,
    load32,
    out32,
    far,
    upper,
):
    owned, shared, local, windows, modes, inner, cut = sizes
    step = pl.program_id(0)
    count = count_ref[0, 0]
    ipad = up(inner, LANES)
    own = owned // GS - cut

    @pl.when(step == 0)
    def _():
        clear(load32, inner * STEP)
        clear(far, local - owned)
        for k, arrived in enumerate((in0_ref, in1_ref, in2_ref, in3_ref)):
            place(far, slice(k * shared, (k + 1) * shared), arrived[0:shared, :].astype(F32))

    deinterleave(load_ref, load32)
    for half in range(STEP // GS):
        group = step * (STEP // GS) + half
        upper[half, 0:own, :] = window_ref[half, cut:, :]
        upper[half, own:, :] = take(far, pl.ds(group, upper.shape[1] - own, stride=GS)).astype(BF16)
        pulled = tn(low_ref[half], window_ref[half, 0:cut, :]) + tn(high_ref[half], upper[half])
        for p in range(GS // 2):
            slot = half * GS + 2 * p
            loads = jnp.concatenate(
                [take(load32, pl.ds(slot + j, ipad, stride=STEP)) for j in range(2)], axis=0
            )
            reduced = (loads - pulled[2 * p * ipad : (2 * p + 2) * ipad]).astype(BF16)
            result = nn(pairs_ref[slot // 2], reduced)
            for j in range(2):
                live = group * GS + 2 * p + j < count
                part = jnp.where(live, result[j * ipad : (j + 1) * ipad], 0.0)
                place(out32, pl.ds(slot + j, ipad, stride=STEP), part)
    for tile in range(2):
        block = out32[tile, 0 : inner * STEP, :].reshape(inner, STEP, LANES)
        out_ref[:, :, tile * LANES : (tile + 1) * LANES] = block.astype(BF16)


def whole(shape):
    zeros = (0,) * len(shape)
    return pl.BlockSpec(shape, lambda *step: zeros)


def by_slot(rows, cols):
    return pl.BlockSpec((rows, STEP, cols), lambda step: (0, step, 0))


def by_lead(lead, *rest):
    return pl.BlockSpec((lead,) + rest, lambda step: (step,) + (0,) * len(rest))


def per_device(
    coupling,
    interior_inverse,
    interior_load,
    boundary_load,
    owner_weight,
    elem_weight,
    elem_dof,
    reader_rows,
    elem_count,
):
    coupling = jnp.transpose(coupling[0, 0], (1, 0, 2))
    inverse = jnp.transpose(interior_inverse[0, 0], (1, 0, 2))
    load = jnp.transpose(interior_load[0, 0], (1, 0, 2))
    edge_load = boundary_load[0, 0]
    owner = owner_weight[0, 0].reshape(-1, LANES)
    weight = elem_weight[0, 0]
    dof = elem_dof[0, 0]
    readers = reader_rows[0, 0]

    modes, slots, inner = coupling.shape
    columns = load.shape[-1]
    owned = edge_load.shape[0]
    shared = readers.shape[1]
    local = owned + 4 * shared
    windows = local // GS
    cut = owned // GS // 256 * 256
    high = up(windows, 16) - cut
    sp = up(shared, 16)
    mpad = up(modes, 16)
    ipad = up(inner, LANES)
    sizes = (owned, shared, local, windows, modes, inner, cut)
    steps = slots // STEP
    groups = slots // GS
    pg = STEP // GS
    smem = pl.BlockSpec(memory_space=pltpu.SMEM)
    params = pltpu.CompilerParams(vmem_limit_bytes=60 * 2**20)
    shape = jax.ShapeDtypeStruct

    pairs, coup, solved, op_high, head, headw, *pays = pl.pallas_call(
        functools.partial(solve_kernel, sizes),
        grid=(steps,),
        in_specs=[
            smem,
            whole(dof.shape),
            whole(weight.shape),
            by_slot(inner, columns),
            by_slot(modes, inner),
            by_slot(inner, inner),
        ],
        out_specs=[
            by_lead(STEP // 2, 2 * ipad, 2 * ipad),
            by_lead(STEP, mpad, LANES),
            by_lead(pg, GS * ipad, columns),
            by_lead(pg, high, GS * ipad),
            whole((2, owned - cut * GS, LANES)),
            whole((owned - cut * GS, LANES)),
        ]
        + [whole((sp, 384))] * 4,
        out_shape=[
            shape((slots // 2, 2 * ipad, 2 * ipad), BF16),
            shape((slots, mpad, LANES), BF16),
            shape((groups, GS * ipad, columns), BF16),
            shape((groups, high, GS * ipad), BF16),
            shape((2, owned - cut * GS, LANES), F32),
            shape((owned - cut * GS, LANES), F32),
        ]
        + [shape((sp, 384), BF16)] * 4,
        scratch_shapes=[
            pltpu.VMEM((slots, 256), jnp.int32),
            pltpu.VMEM((slots, 256), F32),
            pltpu.VMEM((2, ipad * STEP, LANES), F32),
            pltpu.VMEM((1, mpad * STEP, LANES), F32),
            pltpu.VMEM((1, ipad * STEP, LANES), F32),
            pltpu.VMEM((2, high * GS, LANES), F32),
            pltpu.VMEM((high * GS, LANES), F32),
        ],
        compiler_params=params,
        name="solve",
    )(elem_count, dof, weight, load, coupling, inverse)

    def exchanged(blocks):
        return [
            passed_along(blocks[1], "px", 1),
            passed_along(blocks[0], "px", -1),
            passed_along(blocks[3], "py", 1),
            passed_along(blocks[2], "py", -1),
        ]

    arrived = exchanged(pays)

    op_low, total, totalw, picked = pl.pallas_call(
        functools.partial(owned_kernel, sizes),
        grid=(steps,),
        in_specs=[
            smem,
            smem,
            whole(dof.shape),
            whole(weight.shape),
            whole(owner.shape),
            whole(edge_load.shape),
            whole(head.shape),
            whole(headw.shape),
            by_lead(STEP, mpad, LANES),
            by_lead(pg, GS * ipad, columns),
        ],
        out_specs=[
            by_lead(pg, cut, GS * ipad),
            whole((2, owned, LANES)),
            whole((owned, LANES)),
            whole((3, 4 * sp, LANES)),
        ],
        out_shape=[
            shape((groups, cut, GS * ipad), BF16),
            shape((2, owned, LANES), F32),
            shape((owned, LANES), F32),
            shape((3, 4 * sp, LANES), F32),
        ],
        scratch_shapes=[pltpu.VMEM((slots, 256), jnp.int32), pltpu.VMEM((slots, 256), F32)],
        compiler_params=params,
        cost_estimate=pl.CostEstimate(flops=20_000_000_000, bytes_accessed=30_000_000, transcendentals=0),
        name="owned",
    )(elem_count, readers, dof, weight, owner, edge_load, head, headw, coup, solved)

    shares, *sends = pl.pallas_call(
        shares_kernel,
        out_shape=[shape((2, 4 * sp, LANES), F32)] + [shape((sp, columns), BF16)] * 4,
        compiler_params=params,
        name="shares",
    )(picked, *arrived)
    returned = exchanged(sends)

    face, window = pl.pallas_call(
        functools.partial(face_kernel, sizes),
        in_specs=[smem, whole(total.shape), whole(totalw.shape), whole(shares.shape)],
        out_shape=[shape((owned, columns), F32), shape((groups, owned // GS, columns), BF16)],
        scratch_shapes=[pltpu.VMEM((2, owned, LANES), F32)],
        compiler_params=params,
        cost_estimate=pl.CostEstimate(flops=5_000_000_000, bytes_accessed=16_000_000, transcendentals=0),
        name="face",
    )(readers, total, totalw, shares)

    interior = pl.pallas_call(
        functools.partial(recover_kernel, sizes),
        grid=(steps,),
        in_specs=[smem]
        + [whole((sp, columns))] * 4
        + [
            by_lead(pg, owned // GS, columns),
            by_lead(pg, cut, GS * ipad),
            by_lead(pg, high, GS * ipad),
            by_slot(inner, columns),
            by_lead(STEP // 2, 2 * ipad, 2 * ipad),
        ],
        out_specs=by_slot(inner, columns),
        out_shape=shape((inner, slots, columns), BF16),
        scratch_shapes=[
            pltpu.VMEM((2, ipad * STEP, LANES), F32),
            pltpu.VMEM((2, ipad * STEP, LANES), F32),
            pltpu.VMEM((2, up(windows, 16) * GS - owned, LANES), F32),
            pltpu.VMEM((pg, high, columns), BF16),
        ],
        compiler_params=params,
        name="recover",
    )(elem_count, *returned, window, op_low, op_high, load, pairs)
    interior = jnp.transpose(interior, (1, 0, 2))
    return (face[None, None], interior[None, None])


def solution(mesh):
    in_specs = (
        P("px", "py", None, None, None),
        P("px", "py", None, None, None),
        P("px", "py", None, None, None),
        P("px", "py", None, None),
        P("px", "py", None),
        P("px", "py", None, None),
        P("px", "py", None, None),
        P("px", "py", None, None),
        P("px", "py"),
    )
    out_specs = (P("px", "py", None, None), P("px", "py", None, None, None))
    return jax.shard_map(
        per_device, mesh=mesh, in_specs=in_specs, out_specs=out_specs, check_vma=False
    )
```

time: 138 us -> 94.5 us (0.68)
  the two profiles are of different devices: /device:TPU:1 before, /device:TPU:0 now
where the time goes in v1:
time: 94.5 us; the launch traced here: 94.4 us
  Pallas kernels  73.4 us (78%)
  starting transfers between devices  17.2 us (18%)
  local copies, waits for them, and re-layouts  1.7 us (2%)
  between operations  1.42 us (2%)
    pallas_call x1, Pallas kernels, per_device(): pl.pallas_call(functools.partial(owned_kernel, sizes), grid=(steps,), in_...  24.3 us
    pallas_call x1, Pallas kernels, per_device(): pl.pallas_call(functools.partial(solve_kernel, sizes), grid=(steps,), in_...  18.2 us
    ppermute x8, starting transfers between devices, passed_along(): return lax.ppermute(value, axis, pairs)  17.2 us
    pallas_call x1, Pallas kernels, per_device(): pl.pallas_call(functools.partial(recover_kernel, sizes), grid=(steps,), i...  16.8 us
    pallas_call x1, Pallas kernels, per_device(): pl.pallas_call(functools.partial(face_kernel, sizes), in_specs=[smem, who...  10.7 us
    pallas_call x1, Pallas kernels, per_device(): pl.pallas_call(shares_kernel, out_shape=[shape((2, 4 * sp, LANES), F32)]...  3.37 us
  transfers between devices with their start and end apart: 8, of which 0 were waited for; matrix products, arithmetic and copies ran while one was open for 1% of the time, Pallas kernels for 37%

profile of v1, /device:TPU:0, one launch (start us, length us, event | category | flops | bytes accessed | tf_op | source)
XLA Modules:
  0.0 94.4 jit_solution(13567130760894146542)
XLA Ops:
  1.3 18.2 %solve.1 = (bf16[32,256,256]{2,1,0:T(8,128)(2,1)}, bf16[64,224,128]{2,1,0:T(8,128)(2,1)}, bf16[8,1024,256]{2,1,0:T(8,128)(2,1)}, bf16[8,240,1024]{2,1,0:T(8,128)...) custom-call(s32[1,1]{1,0:T(1,128)S(6)} %copy.11.count_ref, ...), custom_call_target="tpu_custom_call" | custom-call | tf_op jit(solution)/shard_map/solve/pallas_call | solution.py:398
  19.4 0.0 collective-permute-start
  19.5 3.6 %collective-permute-start.1 = (bf16[352,384]{1,0:T(8,128)(2,1)}, bf16[352,384]{1,0:T(8,128)(2,1)S(1)}, u32[]{:S(2)}, u32[]{:S(2)}) collective-permute-start(bf16[352,384]{1,0:T(8,128)(2,1)} %get-tuple-element.31), channel_id=1, source_target_pairs={{0,112},{16,0},{32,16},{48,32},{64,48},{80,64},{96,80},{112,96},{1... | collective-permute-start | bytes 811016 | tf_op jit(solution)/shard_map/ppermute | solution.py:24
  23.0 1.6 %collective-permute-start.2 = (bf16[352,384]{1,0:T(8,128)(2,1)}, bf16[352,384]{1,0:T(8,128)(2,1)S(1)}, u32[]{:S(2)}, u32[]{:S(2)}) collective-permute-start(bf16[352,384]{1,0:T(8,128)(2,1)} %get-tuple-element.32), channel_id=1, source_target_pairs={{0,1},{1,2},{2,3},{3,4},{4,5},{5,6},{6,7},{7,8},{8,9},{9,10},{10,1... | collective-permute-start | bytes 811016 | tf_op jit(solution)/shard_map/ppermute | solution.py:24
  24.6 3.8 %collective-permute-start.3 = (bf16[352,384]{1,0:T(8,128)(2,1)}, bf16[352,384]{1,0:T(8,128)(2,1)S(1)}, u32[]{:S(2)}, u32[]{:S(2)}) collective-permute-start(bf16[352,384]{1,0:T(8,128)(2,1)} %get-tuple-element.33), channel_id=1, source_target_pairs={{0,15},{1,0},{2,1},{3,2},{4,3},{5,4},{6,5},{7,6},{8,7},{9,8},{10,9... | collective-permute-start | bytes 811016 | tf_op jit(solution)/shard_map/ppermute | solution.py:24
  28.4 0.6 reduce
  29.0 24.3 %owned.1 = (bf16[8,512,1024]{2,1,0:T(8,128)(2,1)}, f32[2,4608,128]{2,1,0:T(8,128)}, f32[4608,128]{1,0:T(8,128)}, f32[3,1408,128]{2,1,0:T(8,128)}) custom-call(s32[1,1]{1,0:T(1,128)S(6)} %copy.11.count_ref, s32[4,348]{1,0:T(4,128)} %bitcast.29, s32[64,218]{1,0:T(8,128)} %bitcast.24, f32[64,218]{1,0:T(8,128)} %bitcast.26, f32[36,128]{1,0:T(8,128)} %bitcast.27, ...), custom_call_target="tpu_custom_call" | custom-call | flops 20000000000 | bytes 30000000 | tf_op jit(solution)/shard_map/owned/pallas_call | solution.py:450
  53.4 0.0 collective-permute-done.in0_ref
  53.4 0.0 copy-start
  53.4 0.0 collective-permute-done.1.in1_ref
  53.4 0.0 copy-start.1
  53.4 0.0 collective-permute-done.2.in2_ref
  53.4 0.0 collective-permute-done.3.in3_ref
  53.5 0.6 copy-done
  54.1 0.1 copy-done.1
  54.2 0.1 copy-done.2
  54.3 0.1 copy-done.3
  54.4 3.4 %shares.1 = (f32[2,1408,128]{2,1,0:T(8,128)}, bf16[352,256]{1,0:T(8,128)(2,1)}, bf16[352,256]{1,0:T(8,128)(2,1)}, bf16[352,256]{1,0:T(8,128)(2,1)}, bf16[352,256]{1,0:T(8,128)(2,1)}) custom-call(f32[3,1408,128]{2,1,0:T(8,128)} %get-tuple-element.29.picked_ref, bf16[352,384]{1,0:T(8,128)(2,1)} %copy-done, bf16[352,384]{1,0:T(8,128)(2,1)} %copy-done.1, ...), custom_call_target="tpu_custom_call" | custom-call | tf_op jit(solution)/shard_map/shares/pallas_call | solution.py:483
  57.7 0.0 collective-permute-start.4
  57.7 3.0 %collective-permute-start.5 = (bf16[352,256]{1,0:T(8,128)(2,1)}, bf16[352,256]{1,0:T(8,128)(2,1)S(1)}, u32[]{:S(2)}, u32[]{:S(2)}) collective-permute-start(bf16[352,256]{1,0:T(8,128)(2,1)} %get-tuple-element.37), channel_id=1, source_target_pairs={{0,112},{16,0},{32,16},{48,32},{64,48},{80,64},{96,80},{112,96},{1... | collective-permute-start | bytes 540680 | tf_op jit(solution)/shard_map/ppermute | solution.py:24
  60.7 0.0 collective-permute-start.6
  60.7 5.3 %collective-permute-start.7 = (bf16[352,256]{1,0:T(8,128)(2,1)}, bf16[352,256]{1,0:T(8,128)(2,1)S(1)}, u32[]{:S(2)}, u32[]{:S(2)}) collective-permute-start(bf16[352,256]{1,0:T(8,128)(2,1)} %get-tuple-element.39), channel_id=1, source_target_pairs={{0,15},{1,0},{2,1},{3,2},{4,3},{5,4},{6,5},{7,6},{8,7},{9,8},{10,9... | collective-permute-start | bytes 540680 | tf_op jit(solution)/shard_map/ppermute | solution.py:24
  66.0 10.7 %face.1 = (f32[4608,256]{1,0:T(8,128)}, bf16[8,576,256]{2,1,0:T(8,128)(2,1)}) custom-call(s32[4,348]{1,0:T(4,128)} %bitcast.30, f32[2,4608,128]{2,1,0:T(8,128)} %get-tuple-element.27.total_ref, f32[4608,128]{1,0:T(8,128)} %get-tuple-element.28.totalw_ref, f32[2,1408,128]{2,1,0:T(8,128)} %get-tuple-element.34.shares_ref), custom_call_target="tpu_custom_call" | custom-call | flops 5000000000 | bytes 16000000 | tf_op jit(solution)/shard_map/face/pallas_call | solution.py:491
  76.7 0.0 collective-permute-done.4.in0_ref
  76.7 0.0 collective-permute-done.5.in1_ref
  76.7 0.0 collective-permute-done.6.in2_ref
  76.7 0.0 collective-permute-done.7.in3_ref
  76.8 0.6 copy-done.4
  77.4 0.1 copy-done.5
  77.4 0.1 copy-done.6
  77.5 0.1 copy-done.7
  77.6 16.8 %recover.1 = bf16[125,64,256]{2,1,0:T(8,128)(2,1)} custom-call(s32[1,1]{1,0:T(1,128)S(6)} %copy.11.count_ref, bf16[352,256]{1,0:T(8,128)(2,1)} %copy-done.4, bf16[352,256]{1,0:T(8,128)(2,1)} %copy-done.5, bf16[352,256]{1,0:T(8,128)(2,1)} %copy-done.6, bf16[352,256]{1,0:T(8,128)(2,1)} %copy-done.7, bf16[8,576,256]{2,1,0:T(8,128)(2,1)} %get-tuple-element.40.window_ref, ...), custom_call_target="tpu_custom_call" | custom-call | tf_op jit(solution)/shard_map/recover/pallas_call | solution.py:501
  (8 shorter events, 0.0 us)
Async XLA Ops:
  1.3 27.1 %copy-start.8 = (f32[1,1,4608]{2,1,0:T(1,128)S(1)}, f32[1,1,4608]{2,1,0:T(1,128)}, u32[]{:S(2)}) copy-start(f32[1,1,4608]{2,1,0:T(1,128)} %param.13) | copy-start | bytes 55300
  19.4 33.9 %collective-permute-start = (bf16[352,384]{1,0:T(8,128)(2,1)}, bf16[352,384]{1,0:T(8,128)(2,1)S(1)}, u32[]{:S(2)}, u32[]{:S(2)}) collective-permute-start(bf16[352,384]{1,0:T(8,128)(2,1)} %get-tuple-element.30), channel_id=1, source_target_pairs={{0,16},{16,32},{32,48},{48,64},{64,80},{80,96},{96,112},{112,0},{1... | collective-permute-start | bytes 811016 | tf_op jit(solution)/shard_map/ppermute | solution.py:24
  19.5 33.9 %collective-permute-start.1 = (bf16[352,384]{1,0:T(8,128)(2,1)}, bf16[352,384]{1,0:T(8,128)(2,1)S(1)}, u32[]{:S(2)}, u32[]{:S(2)}) collective-permute-start(bf16[352,384]{1,0:T(8,128)(2,1)} %get-tuple-element.31), channel_id=1, source_target_pairs={{0,112},{16,0},{32,16},{48,32},{64,48},{80,64},{96,80},{112,96},{1... | collective-permute-start | bytes 811016 | tf_op jit(solution)/shard_map/ppermute | solution.py:24
  23.0 30.4 %collective-permute-start.2 = (bf16[352,384]{1,0:T(8,128)(2,1)}, bf16[352,384]{1,0:T(8,128)(2,1)S(1)}, u32[]{:S(2)}, u32[]{:S(2)}) collective-permute-start(bf16[352,384]{1,0:T(8,128)(2,1)} %get-tuple-element.32), channel_id=1, source_target_pairs={{0,1},{1,2},{2,3},{3,4},{4,5},{5,6},{6,7},{7,8},{8,9},{9,10},{10,1... | collective-permute-start | bytes 811016 | tf_op jit(solution)/shard_map/ppermute | solution.py:24
  24.6 28.8 %collective-permute-start.3 = (bf16[352,384]{1,0:T(8,128)(2,1)}, bf16[352,384]{1,0:T(8,128)(2,1)S(1)}, u32[]{:S(2)}, u32[]{:S(2)}) collective-permute-start(bf16[352,384]{1,0:T(8,128)(2,1)} %get-tuple-element.33), channel_id=1, source_target_pairs={{0,15},{1,0},{2,1},{3,2},{4,3},{5,4},{6,5},{7,6},{8,7},{9,8},{10,9... | collective-permute-start | bytes 811016 | tf_op jit(solution)/shard_map/ppermute | solution.py:24
  53.4 0.7 copy-start
  53.4 0.8 copy-start.1
  53.4 0.8 copy-start.2
  53.5 0.9 copy-start.3
  57.7 19.0 %collective-permute-start.4 = (bf16[352,256]{1,0:T(8,128)(2,1)}, bf16[352,256]{1,0:T(8,128)(2,1)S(1)}, u32[]{:S(2)}, u32[]{:S(2)}) collective-permute-start(bf16[352,256]{1,0:T(8,128)(2,1)} %get-tuple-element.36), channel_id=1, source_target_pairs={{0,16},{16,32},{32,48},{48,64},{64,80},{80,96},{96,112},{112,0},{1... | collective-permute-start | bytes 540680 | tf_op jit(solution)/shard_map/ppermute | solution.py:24
  57.7 19.0 %collective-permute-start.5 = (bf16[352,256]{1,0:T(8,128)(2,1)}, bf16[352,256]{1,0:T(8,128)(2,1)S(1)}, u32[]{:S(2)}, u32[]{:S(2)}) collective-permute-start(bf16[352,256]{1,0:T(8,128)(2,1)} %get-tuple-element.37), channel_id=1, source_target_pairs={{0,112},{16,0},{32,16},{48,32},{64,48},{80,64},{96,80},{112,96},{1... | collective-permute-start | bytes 540680 | tf_op jit(solution)/shard_map/ppermute | solution.py:24
  60.7 16.0 %collective-permute-start.6 = (bf16[352,256]{1,0:T(8,128)(2,1)}, bf16[352,256]{1,0:T(8,128)(2,1)S(1)}, u32[]{:S(2)}, u32[]{:S(2)}) collective-permute-start(bf16[352,256]{1,0:T(8,128)(2,1)} %get-tuple-element.38), channel_id=1, source_target_pairs={{0,1},{1,2},{2,3},{3,4},{4,5},{5,6},{6,7},{7,8},{8,9},{9,10},{10,1... | collective-permute-start | bytes 540680 | tf_op jit(solution)/shard_map/ppermute | solution.py:24
  60.7 16.1 %collective-permute-start.7 = (bf16[352,256]{1,0:T(8,128)(2,1)}, bf16[352,256]{1,0:T(8,128)(2,1)S(1)}, u32[]{:S(2)}, u32[]{:S(2)}) collective-permute-start(bf16[352,256]{1,0:T(8,128)(2,1)} %get-tuple-element.39), channel_id=1, source_target_pairs={{0,15},{1,0},{2,1},{3,2},{4,3},{5,4},{6,5},{7,6},{8,7},{9,8},{10,9... | collective-permute-start | bytes 540680 | tf_op jit(solution)/shard_map/ppermute | solution.py:24
  76.7 0.7 copy-start.4
  76.7 0.7 copy-start.5
  76.7 0.8 copy-start.6
  76.8 0.8 copy-start.7

commit v2 on v0

v2 whole, which is shorter than its diff:
```python
import functools

import jax
import jax.numpy as jnp
from jax import lax
from jax.experimental import pallas as pl
from jax.experimental.pallas import tpu as pltpu
from jax.sharding import PartitionSpec as P

GS = 8
STEP = 16
LANES = 128
F32 = jnp.float32
BF16 = jnp.bfloat16


def up(value, multiple):
    return -(-value // multiple) * multiple


def passed_along(value, axis, steps):
    count = lax.axis_size(axis)
    pairs = [(source, (source + steps) % count) for source in range(count)]
    return lax.ppermute(value, axis, pairs)


def nn(a, b):
    return lax.dot_general(a, b, (((1,), (0,)), ((), ())), preferred_element_type=F32)


def tn(a, b):
    return lax.dot_general(a, b, (((0,), (0,)), ((), ())), preferred_element_type=F32)


def column_of(row):
    return jnp.transpose(jnp.broadcast_to(row, (LANES, LANES)))


def take(ref, at):
    parts = [ref[tile, at, :] for tile in range(ref.shape[0])]
    return parts[0] if len(parts) == 1 else jnp.concatenate(parts, axis=1)


def place(ref, at, rows):
    for tile in range(ref.shape[0]):
        ref[tile, at, :] = rows[:, tile * LANES : (tile + 1) * LANES]


def deinterleave(source, target):
    rows, slots, cols = source.shape
    for tile in range(target.shape[0]):
        first, end = tile * LANES, min((tile + 1) * LANES, cols)
        block = source[:, :, first:end].astype(F32).reshape(rows * slots, end - first)
        target[tile, 0 : rows * slots, 0 : end - first] = block


def slot_rows(target, slot, rows):
    return take(target, pl.ds(slot, rows, stride=STEP)).astype(BF16)


def clear(ref, first):
    if first < ref.shape[1]:
        ref[:, first:, :] = jnp.zeros((ref.shape[0], ref.shape[1] - first, ref.shape[2]), ref.dtype)


def split(rows):
    top = rows.astype(BF16).astype(F32)
    return jnp.concatenate([top, rows - top], axis=1)


def condense_kernel(
    sizes,
    count_ref,
    readers_ref,
    dof_ref,
    weight_ref,
    owner_ref,
    edge_ref,
    load_ref,
    coupling_ref,
    inverse_ref,
    pairs_ref,
    op_ref,
    total_ref,
    totalw_ref,
    picked_ref,
    pay0_ref,
    pay1_ref,
    pay2_ref,
    pay3_ref,
    dofp,
    weightp,
    load32,
    coup32,
    inv32,
    solved,
):
    owned, shared, local, windows, modes, inner = sizes
    step = pl.program_id(0)
    mpad, ipad, sp, wide = up(modes, 16), up(inner, LANES), up(shared, 16), up(shared, LANES)
    wpad = op_ref.shape[1]

    @pl.when(step == 0)
    def _():
        clear(load32, inner * STEP)
        coup32[...] = jnp.zeros_like(coup32)
        inv32[...] = jnp.zeros_like(inv32)
        live = lax.broadcasted_iota(jnp.int32, dof_ref.shape, 0) < count_ref[0, 0]
        dofp[...] = jnp.full(dofp.shape, -1, jnp.int32)
        dofp[:, 0:modes] = jnp.where(live, lax.shift_right_arithmetic(dof_ref[...], 3), -1)
        weightp[...] = jnp.zeros_like(weightp)
        weightp[:, 0:modes] = weight_ref[...]
        for q in range(owned // LANES):
            totalw_ref[q * LANES : (q + 1) * LANES, :] = column_of(owner_ref[:, q * LANES : (q + 1) * LANES])
        totalw_ref[owned:, :] = jnp.zeros((totalw_ref.shape[0] - owned, LANES), F32)
        for tile in range(2):
            total_ref[tile, 0:owned, :] = edge_ref[:, tile * LANES : (tile + 1) * LANES].astype(F32)
        clear(total_ref, owned)
        picked_ref[0:2] = jnp.zeros((2,) + picked_ref.shape[1:], F32)
        picked_ref[2] = jnp.ones(picked_ref.shape[1:], F32)

    deinterleave(load_ref, load32)
    deinterleave(coupling_ref, coup32)
    deinterleave(inverse_ref, inv32)

    zeros = jnp.zeros((ipad, LANES), BF16)
    for half in range(STEP // GS):
        group = step * (STEP // GS) + half
        at = pl.ds(pl.multiple_of(group * GS, GS), GS)
        for p in range(GS // 2):
            slot = half * GS + 2 * p
            pair = group * (GS // 2) + p
            upper = jnp.concatenate([slot_rows(inv32, slot, ipad), zeros], axis=1)
            lower = jnp.concatenate([zeros, slot_rows(inv32, slot + 1, ipad)], axis=1)
            both = jnp.concatenate([upper, lower], axis=0)
            pairs_ref[pair] = both
            loads = jnp.concatenate(
                [slot_rows(load32, slot, ipad), slot_rows(load32, slot + 1, ipad)], axis=0
            )
            solved[half, 2 * p * ipad : (2 * p + 2) * ipad, :] = nn(both, loads).astype(BF16)
        totals = operator(
            dofp[at, :],
            weightp[at, :],
            lambda e: slot_rows(coup32, half * GS + e, mpad),
            op_ref.at[group],
            0,
            mpad,
        )
        rows = pl.ds(group, wpad, stride=GS)
        place(total_ref, rows, take(total_ref, rows) - nn(op_ref[group], solved[half]))
        totalw_ref[rows, :] = totalw_ref[rows, :] + totals

    @pl.when(step == pl.num_programs(0) - 1)
    def _():
        batch = 12
        for k in range(4):

            def pick(i, _):
                for j in range(batch):
                    s = i * batch + j
                    row = readers_ref[k, s]
                    picked_ref[0, pl.ds(k * wide + s, 1), :] = total_ref[0, pl.ds(row, 1), :]
                    picked_ref[1, pl.ds(k * wide + s, 1), :] = total_ref[1, pl.ds(row, 1), :]
                    picked_ref[2, pl.ds(k * wide + s, 1), :] = totalw_ref[pl.ds(row, 1), :]
                return 0

            lax.fori_loop(0, shared // batch, pick, 0)

        chunks = wide // LANES
        for k, pay in enumerate((pay0_ref, pay1_ref, pay2_ref, pay3_ref)):
            first = owned + k * shared
            for tile in range(2):
                lane = slice(tile * LANES, (tile + 1) * LANES)
                pay[0:sp, lane] = total_ref[tile, first : first + sp, :].astype(BF16)
                pay[sp : 2 * sp, lane] = picked_ref[tile, k * wide : k * wide + sp, :].astype(BF16)
            lines = [totalw_ref[first + c * LANES : first + (c + 1) * LANES, :] for c in range(chunks)]
            lines += [
                picked_ref[2, k * wide + c * LANES : k * wide + (c + 1) * LANES, :] for c in range(chunks)
            ]
            lines = [jnp.transpose(line)[0:1] for line in lines]
            lines.append(jnp.zeros((16 - 2 * chunks, LANES), F32))
            pay[2 * sp :, :] = split(jnp.concatenate(lines, axis=0)).astype(BF16)


def operator(dofs, weights, coupling_of, target, first, mpad):
    count = target.shape[0]
    block = 16
    parts = []
    for chunk in range(0, count, block):
        ids = lax.broadcasted_iota(jnp.int32, (block, 256), 0) + (first + chunk)
        total = jnp.zeros((block, 256), F32)
        for e in range(GS):
            hit = ids == jnp.broadcast_to(dofs[e : e + 1], (block, 256))
            total = total + jnp.where(hit, jnp.broadcast_to(weights[e : e + 1], (block, 256)), 0.0)
        parts.append(total)
    ids = lax.broadcasted_iota(jnp.int32, (count, 256), 0) + first
    for e in range(GS):
        hit = jnp.where(ids == jnp.broadcast_to(dofs[e : e + 1], (count, 256)), 1.0, 0.0).astype(BF16)
        target[:, e * LANES : (e + 1) * LANES] = nn(hit[:, 0:mpad], coupling_of(e)).astype(BF16)
    total = jnp.concatenate(parts, axis=0)
    return jnp.broadcast_to(jnp.sum(total, axis=1, keepdims=True), (count, LANES))


def divide_kernel(owned, total_ref, totalw_ref, out_ref):
    size = 256

    def divide(q, _):
        at = pl.ds(pl.multiple_of(q * size, size), size)
        inverse = 1.0 / totalw_ref[at, :]
        for tile in range(2):
            out_ref[tile, at, :] = total_ref[tile, at, :] * inverse
        return 0

    lax.fori_loop(0, owned // size, divide, 0)


def recover_kernel(
    sizes,
    count_ref,
    readers_ref,
    in0_ref,
    in1_ref,
    in2_ref,
    in3_ref,
    total_ref,
    totalw_ref,
    picked_ref,
    op_ref,
    pairs_ref,
    load_ref,
    face_ref,
    out_ref,
    values,
    load32,
    out32,
    shares,
    out_sem,
):
    owned, shared, local, windows, modes, inner = sizes
    step = pl.program_id(0)
    count = count_ref[0, 0]
    ipad, sp, wide = up(inner, LANES), up(shared, 16), up(shared, LANES)
    wpad = op_ref.shape[1]
    chunks = wide // LANES

    def stores():
        return [
            pltpu.make_async_copy(
                values.at[tile, pl.ds(0, owned)],
                face_ref.at[:, pl.ds(tile * LANES, LANES)],
                out_sem.at[tile],
            )
            for tile in range(2)
        ]

    @pl.when(step == 0)
    def _():
        clear(load32, inner * STEP)
        for k, inc in enumerate((in0_ref, in1_ref, in2_ref, in3_ref)):
            first = owned + k * shared
            sums = inc[2 * sp :, :].astype(F32)
            sums = sums[:, 0:LANES] + sums[:, LANES:]
            columns = [column_of(sums[c : c + 1]) for c in range(2 * chunks)]
            theirs = jnp.concatenate(columns[:chunks], axis=0)[0:shared]
            inverse = 1.0 / (picked_ref[2, k * wide : k * wide + shared, :] + theirs)
            far = jnp.concatenate(columns[chunks:], axis=0)[0:shared]
            inverse_far = 1.0 / (far + totalw_ref[first : first + shared, :])
            for tile in range(2):
                lane = slice(tile * LANES, (tile + 1) * LANES)
                mine = picked_ref[tile, k * wide : k * wide + shared, :]
                shares[tile, k * sp : k * sp + shared, :] = (mine + inc[0:shared, lane].astype(F32)) * inverse
                sent = values[tile, first : first + shared, :]
                values[tile, first : first + shared, :] = (
                    inc[sp : sp + shared, lane].astype(F32) + sent
                ) * inverse_far
        batch = 12
        for k in range(4):

            def put(i, _):
                for j in range(batch):
                    s = i * batch + j
                    row = readers_ref[k, s]
                    for tile in range(2):
                        values[tile, pl.ds(row, 1), :] = shares[tile, pl.ds(k * sp + s, 1), :]
                return 0

            lax.fori_loop(0, shared // batch, put, 0)
        for copy in stores():
            copy.start()

    deinterleave(load_ref, load32)
    for half in range(STEP // GS):
        group = step * (STEP // GS) + half
        window = take(values, pl.ds(group, wpad, stride=GS)).astype(BF16)
        pulled = tn(op_ref[group], window)
        for p in range(GS // 2):
            slot = half * GS + 2 * p
            loads = jnp.concatenate(
                [take(load32, pl.ds(slot + j, ipad, stride=STEP)) for j in range(2)], axis=0
            )
            reduced = (loads - pulled[2 * p * ipad : (2 * p + 2) * ipad]).astype(BF16)
            result = nn(pairs_ref[group * (GS // 2) + p], reduced)
            for j in range(2):
                live = group * GS + 2 * p + j < count
                part = jnp.where(live, result[j * ipad : (j + 1) * ipad], 0.0)
                place(out32, pl.ds(slot + j, ipad, stride=STEP), part)
    for tile in range(2):
        block = out32[tile, 0 : inner * STEP, :].reshape(inner, STEP, LANES)
        out_ref[:, :, tile * LANES : (tile + 1) * LANES] = block.astype(BF16)

    @pl.when(step == pl.num_programs(0) - 1)
    def _():
        for copy in stores():
            copy.wait()


def whole(shape):
    zeros = (0,) * len(shape)
    return pl.BlockSpec(shape, lambda *step: zeros)


def by_slot(rows, cols):
    return pl.BlockSpec((rows, STEP, cols), lambda step: (0, step, 0))


def per_device(
    coupling,
    interior_inverse,
    interior_load,
    boundary_load,
    owner_weight,
    elem_weight,
    elem_dof,
    reader_rows,
    elem_count,
):
    far = lambda value: pltpu.with_memory_space_constraint(value, pltpu.HBM)
    coupling = far(jnp.transpose(coupling[0, 0], (1, 0, 2)))
    inverse = far(jnp.transpose(interior_inverse[0, 0], (1, 0, 2)))
    load = far(jnp.transpose(interior_load[0, 0], (1, 0, 2)))
    edge_load = far(boundary_load[0, 0])
    owner = far(owner_weight[0])
    weight = far(elem_weight[0, 0])
    dof = far(elem_dof[0, 0])
    readers = reader_rows[0, 0]

    modes, slots, inner = coupling.shape
    columns = load.shape[-1]
    owned = edge_load.shape[0]
    shared = readers.shape[1]
    local = owned + 4 * shared
    windows = local // GS
    wpad = up(windows, 16)
    sp, wide = up(shared, 16), up(shared, LANES)
    mpad, ipad = up(modes, 16), up(inner, LANES)
    nat = up(max(wpad * GS, owned + 3 * shared + wide), 16)
    sizes = (owned, shared, local, windows, modes, inner)
    steps = slots // STEP
    groups = slots // GS
    smem = pl.BlockSpec(memory_space=pltpu.SMEM)
    near = pl.BlockSpec(memory_space=pltpu.VMEM)
    shape = jax.ShapeDtypeStruct

    pairs, operators, total, totalw, picked, *pays = pl.pallas_call(
        functools.partial(condense_kernel, sizes),
        grid=(steps,),
        in_specs=[
            smem,
            smem,
            whole(dof.shape),
            whole(weight.shape),
            whole(owner.shape),
            whole(edge_load.shape),
            by_slot(inner, columns),
            by_slot(modes, inner),
            by_slot(inner, inner),
        ],
        out_specs=[near] * 9,
        out_shape=[
            pltpu.VMEM((slots // 2, 2 * ipad, 2 * ipad), BF16),
            pltpu.VMEM((groups, wpad, GS * ipad), BF16),
            pltpu.VMEM((2, nat, LANES), F32),
            pltpu.VMEM((nat, LANES), F32),
            pltpu.VMEM((3, 4 * wide, LANES), F32),
        ]
        + [pltpu.VMEM((2 * sp + 16, columns), BF16)] * 4,
        scratch_shapes=[
            pltpu.VMEM((slots, 256), jnp.int32),
            pltpu.VMEM((slots, 256), F32),
            pltpu.VMEM((2, ipad * STEP, LANES), F32),
            pltpu.VMEM((1, mpad * STEP, LANES), F32),
            pltpu.VMEM((1, ipad * STEP, LANES), F32),
            pltpu.VMEM((STEP // GS, GS * ipad, columns), BF16),
        ],
        compiler_params=pltpu.CompilerParams(vmem_limit_bytes=24 * 2**20),
        name="condense",
    )(elem_count, readers, dof, weight, owner, edge_load, load, coupling, inverse)

    arrived = [
        passed_along(pays[1], "px", 1),
        passed_along(pays[0], "px", -1),
        passed_along(pays[3], "py", 1),
        passed_along(pays[2], "py", -1),
    ]

    total = pl.pallas_call(
        functools.partial(divide_kernel, owned),
        in_specs=[near, near],
        out_specs=near,
        out_shape=pltpu.VMEM((2, nat, LANES), F32),
        input_output_aliases={0: 0},
        cost_estimate=pl.CostEstimate(flops=2_000_000_000, bytes_accessed=12_000_000, transcendentals=0),
        compiler_params=pltpu.CompilerParams(vmem_limit_bytes=8 * 2**20),
        name="divide",
    )(total, totalw)

    face, interior, _ = pl.pallas_call(
        functools.partial(recover_kernel, sizes),
        grid=(steps,),
        in_specs=[smem, smem] + [near] * 9 + [by_slot(inner, columns)],
        out_specs=[pl.BlockSpec(memory_space=pltpu.HBM), by_slot(inner, columns), near],
        out_shape=[
            pltpu.HBM((owned, columns), F32),
            pltpu.HBM((inner, slots, columns), BF16),
            pltpu.VMEM((2, nat, LANES), F32),
        ],
        input_output_aliases={6: 2},
        scratch_shapes=[
            pltpu.VMEM((2, ipad * STEP, LANES), F32),
            pltpu.VMEM((2, ipad * STEP, LANES), F32),
            pltpu.VMEM((2, 4 * sp, LANES), F32),
            pltpu.SemaphoreType.DMA((2,)),
        ],
        compiler_params=pltpu.CompilerParams(vmem_limit_bytes=23 * 2**20),
        name="recover",
    )(elem_count, readers, *arrived, total, totalw, picked, operators, pairs, load)
    interior = jnp.transpose(interior, (1, 0, 2))
    return (face[None, None], interior[None, None])


def solution(mesh):
    in_specs = (
        P("px", "py", None, None, None),
        P("px", "py", None, None, None),
        P("px", "py", None, None, None),
        P("px", "py", None, None),
        P("px", "py", None),
        P("px", "py", None, None),
        P("px", "py", None, None),
        P("px", "py", None, None),
        P("px", "py"),
    )
    out_specs = (P("px", "py", None, None), P("px", "py", None, None, None))
    return jax.shard_map(
        per_device, mesh=mesh, in_specs=in_specs, out_specs=out_specs, check_vma=False
    )
```

time: 138 us -> 69 us (0.50)
  the two profiles are of different devices: /device:TPU:1 before, /device:TPU:0 now
where the time goes in v2:
time: 69 us; the launch traced here: 68.8 us
  Pallas kernels  51.5 us (75%)
  starting transfers between devices  8.94 us (13%)
  waiting for transfers between devices  6.41 us (9%)
  between operations  1.33 us (2%)
    pallas_call x1, Pallas kernels, per_device(): pl.pallas_call(functools.partial(condense_kernel, sizes), grid=(steps,),...  31.6 us
    pallas_call x1, Pallas kernels, per_device(): pl.pallas_call(functools.partial(recover_kernel, sizes), grid=(steps,), i...  19.2 us
    ppermute x4, starting transfers between devices, passed_along(): return lax.ppermute(value, axis, pairs)  8.94 us
    ppermute x4, waiting for transfers between devices, passed_along(): return lax.ppermute(value, axis, pairs)  6.41 us
  transfers between devices with their start and end apart: 4, of which 1 were waited for; matrix products, arithmetic and copies ran while one was open for 0% of the time, Pallas kernels for 1%

profile of v2, /device:TPU:0, one launch (start us, length us, event | category | flops | bytes accessed | tf_op | source)
XLA Modules:
  0.0 68.8 jit_solution(16940959208690668842)
XLA Ops:
  1.3 0.0 copy-start
  1.3 0.7 copy-done
  2.0 31.6 %condense.1 = (bf16[32,256,256]{2,1,0:T(8,128)(2,1)S(1)}, bf16[8,752,1024]{2,1,0:T(8,128)(2,1)S(1)}, f32[2,6048,128]{2,1,0:T(8,128)S(1)}, f32[6048,128]{1,0:T(8,...) custom-call(s32[1,1]{1,0:T(1,128)S(6)} %copy.15.count_ref, ...), custom_call_target="tpu_custom_call" | custom-call | tf_op jit(solution)/shard_map/condense/pallas_call | solution.py:364
  33.6 0.0 collective-permute-start
  33.6 3.6 %collective-permute-start.1 = (bf16[720,256]{1,0:T(8,128)(2,1)S(1)}, bf16[720,256]{1,0:T(8,128)(2,1)S(1)}, u32[]{:S(2)}, u32[]{:S(2)}) collective-permute-start(bf16[720,256]{1,0:T(8,128)(2,1)S(1)} %get-tuple-element.14), channel_id=1, source_target_pairs={{0,112},{16,0},{32,16},{48,32},{64,48},{80,64},{96,80},{112,96},{1... | collective-permute-start | bytes 1105928 | tf_op jit(solution)/shard_map/ppermute | solution.py:24
  37.2 1.6 %collective-permute-start.2 = (bf16[720,256]{1,0:T(8,128)(2,1)S(1)}, bf16[720,256]{1,0:T(8,128)(2,1)S(1)}, u32[]{:S(2)}, u32[]{:S(2)}) collective-permute-start(bf16[720,256]{1,0:T(8,128)(2,1)S(1)} %get-tuple-element.15), channel_id=1, source_target_pairs={{0,1},{1,2},{2,3},{3,4},{4,5},{5,6},{6,7},{7,8},{8,9},{9,10},{10,1... | collective-permute-start | bytes 1105928 | tf_op jit(solution)/shard_map/ppermute | solution.py:24
  38.7 3.8 %collective-permute-start.3 = (bf16[720,256]{1,0:T(8,128)(2,1)S(1)}, bf16[720,256]{1,0:T(8,128)(2,1)S(1)}, u32[]{:S(2)}, u32[]{:S(2)}) collective-permute-start(bf16[720,256]{1,0:T(8,128)(2,1)S(1)} %get-tuple-element.16), channel_id=1, source_target_pairs={{0,15},{1,0},{2,1},{3,2},{4,3},{5,4},{6,5},{7,6},{8,7},{9,8},{10,9... | collective-permute-start | bytes 1105928 | tf_op jit(solution)/shard_map/ppermute | solution.py:24
  42.5 0.7 %divide.1.total_ref = f32[2,6048,128]{2,1,0:T(8,128)S(1)} custom-call(f32[2,6048,128]{2,1,0:T(8,128)S(1)} %get-tuple-element.17.total_ref, f32[6048,128]{1,0:T(8,128)S(1)} %get-tuple-element.18.totalw_ref), custom_call_target="tpu_custom_call", output_to_operand_aliasing={{}: (0, {})} | custom-call | flops 2000000000 | bytes 12000000 | tf_op jit(solution)/shard_map/divide/pallas_call | solution.py:406
  43.2 0.0 collective-permute-done.in0_ref
  43.2 0.0 collective-permute-done.1.in1_ref
  43.3 6.4 %collective-permute-done.2.in2_ref = bf16[720,256]{1,0:T(8,128)(2,1)S(1)} collective-permute-done((bf16[720,256]{1,0:T(8,128)(2,1)S(1)}, bf16[720,256]{1,0:T(8,128)(2,1)S(1)}, u32[]{:S(2)}, u32[]{:S(2)}) %collective-permute-start.2) | collective-permute-done | bytes 368672 | tf_op jit(solution)/shard_map/ppermute | solution.py:24
  49.7 0.0 collective-permute-done.3.in3_ref
  49.7 19.2 %recover.1 = (f32[4608,256]{1,0:T(8,128)}, bf16[125,64,256]{2,1,0:T(8,128)(2,1)}, f32[2,6048,128]{2,1,0:T(8,128)S(1)}) custom-call(s32[1,1]{1,0:T(1,128)S(6)} %copy.15.count_ref, s32[4,348]{1,0:T(4,128)S(1)} %bitcast.19, bf16[720,256]{1,0:T(8,128)(2,1)S(1)} %collective-permute-done.in0_ref, ...), custom_call_target="tpu_custom_call", output_to_operand_aliasing={{2}: (6, {})} | custom-call | tf_op jit(solution)/shard_map/recover/pallas_call | solution.py:417
Async XLA Ops:
  1.3 0.7 %copy-start = (s32[1,1,4,348]{3,2,1,0:T(4,128)S(1)}, s32[1,1,4,348]{3,2,1,0:T(4,128)}, u32[]{:S(2)}) copy-start(s32[1,1,4,348]{3,2,1,0:T(4,128)} %param.16) | copy-start | bytes 16708
  33.6 9.7 %collective-permute-start = (bf16[720,256]{1,0:T(8,128)(2,1)S(1)}, bf16[720,256]{1,0:T(8,128)(2,1)S(1)}, u32[]{:S(2)}, u32[]{:S(2)}) collective-permute-start(bf16[720,256]{1,0:T(8,128)(2,1)S(1)} %get-tuple-element.13), channel_id=1, source_target_pairs={{0,16},{16,32},{32,48},{48,64},{64,80},{80,96},{96,112},{112,0},{1... | collective-permute-start | bytes 1105928 | tf_op jit(solution)/shard_map/ppermute | solution.py:24
  33.6 9.6 %collective-permute-start.1 = (bf16[720,256]{1,0:T(8,128)(2,1)S(1)}, bf16[720,256]{1,0:T(8,128)(2,1)S(1)}, u32[]{:S(2)}, u32[]{:S(2)}) collective-permute-start(bf16[720,256]{1,0:T(8,128)(2,1)S(1)} %get-tuple-element.14), channel_id=1, source_target_pairs={{0,112},{16,0},{32,16},{48,32},{64,48},{80,64},{96,80},{112,96},{1... | collective-permute-start | bytes 1105928 | tf_op jit(solution)/shard_map/ppermute | solution.py:24
  37.2 12.5 %collective-permute-start.2 = (bf16[720,256]{1,0:T(8,128)(2,1)S(1)}, bf16[720,256]{1,0:T(8,128)(2,1)S(1)}, u32[]{:S(2)}, u32[]{:S(2)}) collective-permute-start(bf16[720,256]{1,0:T(8,128)(2,1)S(1)} %get-tuple-element.15), channel_id=1, source_target_pairs={{0,1},{1,2},{2,3},{3,4},{4,5},{5,6},{6,7},{7,8},{8,9},{9,10},{10,1... | collective-permute-start | bytes 1105928 | tf_op jit(solution)/shard_map/ppermute | solution.py:24
  38.7 10.9 %collective-permute-start.3 = (bf16[720,256]{1,0:T(8,128)(2,1)S(1)}, bf16[720,256]{1,0:T(8,128)(2,1)S(1)}, u32[]{:S(2)}, u32[]{:S(2)}) collective-permute-start(bf16[720,256]{1,0:T(8,128)(2,1)S(1)} %get-tuple-element.16), channel_id=1, source_target_pairs={{0,15},{1,0},{2,1},{3,2},{4,3},{5,4},{6,5},{7,6},{8,7},{9,8},{10,9... | collective-permute-start | bytes 1105928 | tf_op jit(solution)/shard_map/ppermute | solution.py:24

commit v3 on v2

--- a/solution.py
+++ b/solution.py
@@ -84,8 +84,6 @@
     total_ref,
     totalw_ref,
     picked_ref,
-    pay0_ref,
-    pay1_ref,
     pay2_ref,
     pay3_ref,
     dofp,
@@ -97,7 +95,7 @@
 ):
     owned, shared, local, windows, modes, inner = sizes
     step = pl.program_id(0)
-    mpad, ipad, sp, wide = up(modes, 16), up(inner, LANES), up(shared, 16), up(shared, LANES)
+    mpad, ipad = up(modes, 16), up(inner, LANES)
     wpad = op_ref.shape[1]
 
     @pl.when(step == 0)
@@ -116,8 +114,6 @@
         for tile in range(2):
             total_ref[tile, 0:owned, :] = edge_ref[:, tile * LANES : (tile + 1) * LANES].astype(F32)
         clear(total_ref, owned)
-        picked_ref[0:2] = jnp.zeros((2,) + picked_ref.shape[1:], F32)
-        picked_ref[2] = jnp.ones(picked_ref.shape[1:], F32)
 
     deinterleave(load_ref, load32)
     deinterleave(coupling_ref, coup32)
@@ -141,9 +137,8 @@
         totals = operator(
             dofp[at, :],
             weightp[at, :],
-            lambda e: slot_rows(coup32, half * GS + e, mpad),
+            lambda e: take(coup32, pl.ds(half * GS + e, mpad, stride=STEP)),
             op_ref.at[group],
-            0,
             mpad,
         )
         rows = pl.ds(group, wpad, stride=GS)
@@ -152,53 +147,83 @@
 
     @pl.when(step == pl.num_programs(0) - 1)
     def _():
-        batch = 12
-        for k in range(4):
-
-            def pick(i, _):
-                for j in range(batch):
-                    s = i * batch + j
-                    row = readers_ref[k, s]
-                    picked_ref[0, pl.ds(k * wide + s, 1), :] = total_ref[0, pl.ds(row, 1), :]
-                    picked_ref[1, pl.ds(k * wide + s, 1), :] = total_ref[1, pl.ds(row, 1), :]
-                    picked_ref[2, pl.ds(k * wide + s, 1), :] = totalw_ref[pl.ds(row, 1), :]
-                return 0
-
-            lax.fori_loop(0, shared // batch, pick, 0)
-
-        chunks = wide // LANES
-        for k, pay in enumerate((pay0_ref, pay1_ref, pay2_ref, pay3_ref)):
-            first = owned + k * shared
-            for tile in range(2):
-                lane = slice(tile * LANES, (tile + 1) * LANES)
-                pay[0:sp, lane] = total_ref[tile, first : first + sp, :].astype(BF16)
-                pay[sp : 2 * sp, lane] = picked_ref[tile, k * wide : k * wide + sp, :].astype(BF16)
-            lines = [totalw_ref[first + c * LANES : first + (c + 1) * LANES, :] for c in range(chunks)]
-            lines += [
-                picked_ref[2, k * wide + c * LANES : k * wide + (c + 1) * LANES, :] for c in range(chunks)
-            ]
-            lines = [jnp.transpose(line)[0:1] for line in lines]
-            lines.append(jnp.zeros((16 - 2 * chunks, LANES), F32))
-            pay[2 * sp :, :] = split(jnp.concatenate(lines, axis=0)).astype(BF16)
-
-
-def operator(dofs, weights, coupling_of, target, first, mpad):
+        pack(sizes, (2, 3), (pay2_ref, pay3_ref), readers_ref, total_ref, totalw_ref, picked_ref)
+
+
+def pack(sizes, directions, pays, readers_ref, total_ref, totalw_ref, picked_ref):
+    owned, shared, local, windows, modes, inner = sizes
+    sp, wide = up(shared, 16), up(shared, LANES)
+    chunks = wide // LANES
+    batch = 29
+    for slot, k in enumerate(directions):
+        first = slot * wide + shared
+        picked_ref[0:2, first : first + wide - shared, :] = jnp.zeros((2, wide - shared, LANES), F32)
+        picked_ref[2, first : first + wide - shared, :] = jnp.ones((wide - shared, LANES), F32)
+
+        def pick(i, _):
+            for j in range(batch):
+                s = i * batch + j
+                row = readers_ref[k, s]
+                picked_ref[0, pl.ds(slot * wide + s, 1), :] = total_ref[0, pl.ds(row, 1), :]
+                picked_ref[1, pl.ds(slot * wide + s, 1), :] = total_ref[1, pl.ds(row, 1), :]
+                picked_ref[2, pl.ds(slot * wide + s, 1), :] = totalw_ref[pl.ds(row, 1), :]
+            return 0
+
+        lax.fori_loop(0, shared // batch, pick, 0)
+
+    for slot, (k, pay) in enumerate(zip(directions, pays)):
+        first = owned + k * shared
+        for tile in range(2):
+            lane = slice(tile * LANES, (tile + 1) * LANES)
+            pay[0:sp, lane] = total_ref[tile, first : first + sp, :].astype(BF16)
+            pay[sp : 2 * sp, lane] = picked_ref[tile, slot * wide : slot * wide + sp, :].astype(BF16)
+        lines = [totalw_ref[first + c * LANES : first + (c + 1) * LANES, :] for c in range(chunks)]
+        lines += [
+            picked_ref[2, slot * wide + c * LANES : slot * wide + (c + 1) * LANES, :] for c in range(chunks)
+        ]
+        lines = [jnp.transpose(line)[0:1] for line in lines]
+        lines.append(jnp.zeros((16 - 2 * chunks, LANES), F32))
+        pay[2 * sp :, :] = split(jnp.concatenate(lines, axis=0)).astype(BF16)
+
+
+def pack_kernel(sizes, readers_ref, total_ref, totalw_ref, picked_ref, pay0_ref, pay1_ref):
+    pack(sizes, (0, 1), (pay0_ref, pay1_ref), readers_ref, total_ref, totalw_ref, picked_ref)
+
+
+def weight_columns(row):
+    high = row.astype(BF16).astype(F32)
+    middle = (row - high).astype(BF16).astype(F32)
+    low = row - high - middle
+    lines = lax.broadcasted_iota(jnp.int32, (LANES, 256), 0)
+    packed = jnp.where(lines == LANES - 3, jnp.broadcast_to(high, (LANES, 256)), 0.0)
+    packed = jnp.where(lines == LANES - 2, jnp.broadcast_to(middle, (LANES, 256)), packed)
+    packed = jnp.where(lines == LANES - 1, jnp.broadcast_to(low, (LANES, 256)), packed)
+    return jnp.transpose(packed)
+
+
+def operator(dofs, weights, coupling_of, target, mpad):
     count = target.shape[0]
-    block = 16
+    block = 256
+    wide = [jnp.broadcast_to(dofs[e : e + 1], (16, 256)).astype(jnp.int16) for e in range(GS)]
+    coup = [
+        (coupling_of(e) + weight_columns(weights[e : e + 1])[0:mpad]).astype(BF16) for e in range(GS)
+    ]
+    base = lax.broadcasted_iota(jnp.int32, (16, 256), 0)
     parts = []
     for chunk in range(0, count, block):
-        ids = lax.broadcasted_iota(jnp.int32, (block, 256), 0) + (first + chunk)
-        total = jnp.zeros((block, 256), F32)
+        size = min(block, count - chunk)
+        ids = jnp.concatenate([(base + (chunk + i)).astype(jnp.int16) for i in range(0, size, 16)], axis=0)
+        one, none = jnp.ones((size, 256), BF16), jnp.zeros((size, 256), BF16)
+        total = jnp.zeros((size, LANES), F32)
         for e in range(GS):
-            hit = ids == jnp.broadcast_to(dofs[e : e + 1], (block, 256))
-            total = total + jnp.where(hit, jnp.broadcast_to(weights[e : e + 1], (block, 256)), 0.0)
-        parts.append(total)
-    ids = lax.broadcasted_iota(jnp.int32, (count, 256), 0) + first
-    for e in range(GS):
-        hit = jnp.where(ids == jnp.broadcast_to(dofs[e : e + 1], (count, 256)), 1.0, 0.0).astype(BF16)
-        target[:, e * LANES : (e + 1) * LANES] = nn(hit[:, 0:mpad], coupling_of(e)).astype(BF16)
-    total = jnp.concatenate(parts, axis=0)
-    return jnp.broadcast_to(jnp.sum(total, axis=1, keepdims=True), (count, LANES))
+            hit = jnp.where(ids == jnp.concatenate([wide[e]] * (size // 16), axis=0), one, none)
+            result = nn(hit[:, 0:mpad], coup[e])
+            target[chunk : chunk + size, e * LANES : (e + 1) * LANES] = result.astype(BF16)
+            total = total + result
+        lanes = lax.broadcasted_iota(jnp.int32, (size, LANES), 1)
+        total = jnp.sum(jnp.where(lanes >= LANES - 3, total, 0.0), axis=1, keepdims=True)
+        parts.append(jnp.broadcast_to(total, (size, LANES)))
+    return jnp.concatenate(parts, axis=0)
 
 
 def divide_kernel(owned, total_ref, totalw_ref, out_ref):
@@ -214,14 +239,51 @@
     lax.fori_loop(0, owned // size, divide, 0)
 
 
+def absorb(sizes, directions, arrivals, readers_ref, totalw_ref, picked_ref, values, shares):
+    owned, shared, local, windows, modes, inner = sizes
+    sp, wide = up(shared, 16), up(shared, LANES)
+    chunks = wide // LANES
+    for slot, (k, inc) in enumerate(zip(directions, arrivals)):
+        first = owned + k * shared
+        sums = inc[2 * sp :, :].astype(F32)
+        sums = sums[:, 0:LANES] + sums[:, LANES:]
+        columns = [column_of(sums[c : c + 1]) for c in range(2 * chunks)]
+        theirs = jnp.concatenate(columns[:chunks], axis=0)[0:shared]
+        inverse = 1.0 / (picked_ref[2, slot * wide : slot * wide + shared, :] + theirs)
+        far = jnp.concatenate(columns[chunks:], axis=0)[0:shared]
+        inverse_far = 1.0 / (far + totalw_ref[first : first + shared, :])
+        for tile in range(2):
+            lane = slice(tile * LANES, (tile + 1) * LANES)
+            mine = picked_ref[tile, slot * wide : slot * wide + shared, :]
+            shares[tile, slot * sp : slot * sp + shared, :] = (mine + inc[0:shared, lane].astype(F32)) * inverse
+            sent = values[tile, first : first + shared, :]
+            values[tile, first : first + shared, :] = (inc[sp : sp + shared, lane].astype(F32) + sent) * inverse_far
+    batch = 29
+    for slot, k in enumerate(directions):
+
+        def put(i, _):
+            for j in range(batch):
+                s = i * batch + j
+                row = readers_ref[k, s]
+                for tile in range(2):
+                    values[tile, pl.ds(row, 1), :] = shares[tile, pl.ds(slot * sp + s, 1), :]
+            return 0
+
+        lax.fori_loop(0, shared // batch, put, 0)
+
+
+def early_kernel(
+    sizes, readers_ref, in2_ref, in3_ref, total_ref, totalw_ref, picked_ref, values, shares
+):
+    absorb(sizes, (2, 3), (in2_ref, in3_ref), readers_ref, totalw_ref, picked_ref, values, shares)
+
+
 def recover_kernel(
     sizes,
     count_ref,
     readers_ref,
     in0_ref,
     in1_ref,
-    in2_ref,
-    in3_ref,
     total_ref,
     totalw_ref,
     picked_ref,
@@ -239,9 +301,8 @@
     owned, shared, local, windows, modes, inner = sizes
     step = pl.program_id(0)
     count = count_ref[0, 0]
-    ipad, sp, wide = up(inner, LANES), up(shared, 16), up(shared, LANES)
+    ipad = up(inner, LANES)
     wpad = op_ref.shape[1]
-    chunks = wide // LANES
 
     def stores():
         return [
@@ -256,35 +317,7 @@
     @pl.when(step == 0)
     def _():
         clear(load32, inner * STEP)
-        for k, inc in enumerate((in0_ref, in1_ref, in2_ref, in3_ref)):
-            first = owned + k * shared
-            sums = inc[2 * sp :, :].astype(F32)
-            sums = sums[:, 0:LANES] + sums[:, LANES:]
-            columns = [column_of(sums[c : c + 1]) for c in range(2 * chunks)]
-            theirs = jnp.concatenate(columns[:chunks], axis=0)[0:shared]
-            inverse = 1.0 / (picked_ref[2, k * wide : k * wide + shared, :] + theirs)
-            far = jnp.concatenate(columns[chunks:], axis=0)[0:shared]
-            inverse_far = 1.0 / (far + totalw_ref[first : first + shared, :])
-            for tile in range(2):
-                lane = slice(tile * LANES, (tile + 1) * LANES)
-                mine = picked_ref[tile, k * wide : k * wide + shared, :]
-                shares[tile, k * sp : k * sp + shared, :] = (mine + inc[0:shared, lane].astype(F32)) * inverse
-                sent = values[tile, first : first + shared, :]
-                values[tile, first : first + shared, :] = (
-                    inc[sp : sp + shared, lane].astype(F32) + sent
-                ) * inverse_far
-        batch = 12
-        for k in range(4):
-
-            def put(i, _):
-                for j in range(batch):
-                    s = i * batch + j
-                    row = readers_ref[k, s]
-                    for tile in range(2):
-                        values[tile, pl.ds(row, 1), :] = shares[tile, pl.ds(k * sp + s, 1), :]
-                return 0
-
-            lax.fori_loop(0, shared // batch, put, 0)
+        absorb(sizes, (0, 1), (in0_ref, in1_ref), readers_ref, totalw_ref, picked_ref, values, shares)
         for copy in stores():
             copy.start()
 
@@ -375,15 +408,15 @@
             by_slot(modes, inner),
             by_slot(inner, inner),
         ],
-        out_specs=[near] * 9,
+        out_specs=[near] * 7,
         out_shape=[
             pltpu.VMEM((slots // 2, 2 * ipad, 2 * ipad), BF16),
             pltpu.VMEM((groups, wpad, GS * ipad), BF16),
             pltpu.VMEM((2, nat, LANES), F32),
             pltpu.VMEM((nat, LANES), F32),
-            pltpu.VMEM((3, 4 * wide, LANES), F32),
+            pltpu.VMEM((3, 2 * wide, LANES), F32),
         ]
-        + [pltpu.VMEM((2 * sp + 16, columns), BF16)] * 4,
+        + [pltpu.VMEM((2 * sp + 16, columns), BF16)] * 2,
         scratch_shapes=[
             pltpu.VMEM((slots, 256), jnp.int32),
             pltpu.VMEM((slots, 256), F32),
@@ -396,12 +429,18 @@
         name="condense",
     )(elem_count, readers, dof, weight, owner, edge_load, load, coupling, inverse)
 
-    arrived = [
-        passed_along(pays[1], "px", 1),
-        passed_along(pays[0], "px", -1),
-        passed_along(pays[3], "py", 1),
-        passed_along(pays[2], "py", -1),
-    ]
+    returned = [passed_along(pays[1], "py", 1), passed_along(pays[0], "py", -1)]
+
+    picked_x, *pays_x = pl.pallas_call(
+        functools.partial(pack_kernel, sizes),
+        in_specs=[smem, near, near],
+        out_specs=[near] * 3,
+        out_shape=[pltpu.VMEM((3, 2 * wide, LANES), F32)] + [pltpu.VMEM((2 * sp + 16, columns), BF16)] * 2,
+        cost_estimate=pl.CostEstimate(flops=5_000_000_000, bytes_accessed=20_000_000, transcendentals=0),
+        compiler_params=pltpu.CompilerParams(vmem_limit_bytes=8 * 2**20),
+        name="pack",
+    )(readers, total, totalw)
+    arrived = [passed_along(pays_x[1], "px", 1), passed_along(pays_x[0], "px", -1)]
 
     total = pl.pallas_call(
         functools.partial(divide_kernel, owned),
@@ -414,26 +453,38 @@
         name="divide",
     )(total, totalw)
 
+    total = pl.pallas_call(
+        functools.partial(early_kernel, sizes),
+        in_specs=[smem] + [near] * 5,
+        out_specs=near,
+        out_shape=pltpu.VMEM((2, nat, LANES), F32),
+        input_output_aliases={3: 0},
+        scratch_shapes=[pltpu.VMEM((2, 2 * sp, LANES), F32)],
+        cost_estimate=pl.CostEstimate(flops=5_000_000_000, bytes_accessed=20_000_000, transcendentals=0),
+        compiler_params=pltpu.CompilerParams(vmem_limit_bytes=8 * 2**20),
+        name="early",
+    )(readers, *returned, total, totalw, picked)
+
     face, interior, _ = pl.pallas_call(
         functools.partial(recover_kernel, sizes),
         grid=(steps,),
-        in_specs=[smem, smem] + [near] * 9 + [by_slot(inner, columns)],
+        in_specs=[smem, smem] + [near] * 7 + [by_slot(inner, columns)],
         out_specs=[pl.BlockSpec(memory_space=pltpu.HBM), by_slot(inner, columns), near],
         out_shape=[
             pltpu.HBM((owned, columns), F32),
             pltpu.HBM((inner, slots, columns), BF16),
             pltpu.VMEM((2, nat, LANES), F32),
         ],
-        input_output_aliases={6: 2},
+        input_output_aliases={4: 2},
         scratch_shapes=[
             pltpu.VMEM((2, ipad * STEP, LANES), F32),
             pltpu.VMEM((2, ipad * STEP, LANES), F32),
-            pltpu.VMEM((2, 4 * sp, LANES), F32),
+            pltpu.VMEM((2, 2 * sp, LANES), F32),
             pltpu.SemaphoreType.DMA((2,)),
         ],
         compiler_params=pltpu.CompilerParams(vmem_limit_bytes=23 * 2**20),
         name="recover",
-    )(elem_count, readers, *arrived, total, totalw, picked, operators, pairs, load)
+    )(elem_count, readers, *arrived, total, totalw, picked_x, operators, pairs, load)
     interior = jnp.transpose(interior, (1, 0, 2))
     return (face[None, None], interior[None, None])
 

time: 69 us -> 61.3 us (0.89)
  the two profiles are of different devices: /device:TPU:0 before, /device:TPU:1 now
where the time goes in v3:
time: 61.3 us; the launch traced here: 61.2 us
  Pallas kernels  47 us (77%)
  starting transfers between devices  8.47 us (14%)
  waiting for transfers between devices  3.68 us (6%)
  between operations  1.33 us (2%)
  local copies, waits for them, and re-layouts  0.68 us (1%)
    pallas_call x1, Pallas kernels, per_device(): pl.pallas_call(functools.partial(condense_kernel, sizes), grid=(steps,),...  24.2 us
    pallas_call x1, Pallas kernels, per_device(): pl.pallas_call(functools.partial(recover_kernel, sizes), grid=(steps,), i...  17 us
    ppermute x4, starting transfers between devices, passed_along(): return lax.ppermute(value, axis, pairs)  8.47 us
    ppermute x4, waiting for transfers between devices, passed_along(): return lax.ppermute(value, axis, pairs)  3.68 us
    pallas_call x1, Pallas kernels, per_device(): pl.pallas_call(functools.partial(pack_kernel, sizes), in_specs=[smem, nea...  2.55 us
    pallas_call x1, Pallas kernels, per_device(): pl.pallas_call(functools.partial(early_kernel, sizes), in_specs=[smem] +...  2.52 us
  transfers between devices with their start and end apart: 4, of which 2 were waited for; matrix products, arithmetic and copies ran while one was open for 0% of the time, Pallas kernels for 9%

profile of v3, /device:TPU:1, one launch (start us, length us, event | category | flops | bytes accessed | tf_op | source)
XLA Modules:
  0.0 61.2 jit_solution(16859895659989939977)
XLA Ops:
  1.3 0.0 copy-start
  1.3 0.7 %copy-done = s32[1,1,4,348]{3,2,1,0:T(4,128)S(1)} copy-done((s32[1,1,4,348]{3,2,1,0:T(4,128)S(1)}, s32[1,1,4,348]{3,2,1,0:T(4,128)}, u32[]{:S(2)}) %copy-start) | copy-done | bytes 5592
  2.0 24.2 %condense.1 = (bf16[32,256,256]{2,1,0:T(8,128)(2,1)S(1)}, bf16[8,752,1024]{2,1,0:T(8,128)(2,1)S(1)}, f32[2,6048,128]{2,1,0:T(8,128)S(1)}, f32[6048,128]{1,0:T(8,...) custom-call(s32[1,1]{1,0:T(1,128)S(6)} %copy.17.count_ref, ...), custom_call_target="tpu_custom_call" | custom-call | tf_op jit(solution)/shard_map/condense/pallas_call | solution.py:397
  26.1 2.2 %collective-permute-start.2 = (bf16[720,256]{1,0:T(8,128)(2,1)S(1)}, bf16[720,256]{1,0:T(8,128)(2,1)S(1)}, u32[]{:S(2)}, u32[]{:S(2)}) collective-permute-start(bf16[720,256]{1,0:T(8,128)(2,1)S(1)} %get-tuple-element.18), channel_id=1, source_target_pairs={{0,1},{1,2},{2,3},{3,4},{4,5},{5,6},{6,7},{7,8},{8,9},{9,10},{10,1... | collective-permute-start | bytes 1105928 | tf_op jit(solution)/shard_map/ppermute | solution.py:24
  28.4 3.7 %collective-permute-start.3 = (bf16[720,256]{1,0:T(8,128)(2,1)S(1)}, bf16[720,256]{1,0:T(8,128)(2,1)S(1)}, u32[]{:S(2)}, u32[]{:S(2)}) collective-permute-start(bf16[720,256]{1,0:T(8,128)(2,1)S(1)} %get-tuple-element.19), channel_id=1, source_target_pairs={{0,15},{1,0},{2,1},{3,2},{4,3},{5,4},{6,5},{7,6},{8,7},{9,8},{10,9... | collective-permute-start | bytes 1105928 | tf_op jit(solution)/shard_map/ppermute | solution.py:24
  32.1 2.6 %pack.1 = (f32[3,768,128]{2,1,0:T(8,128)S(1)}, bf16[720,256]{1,0:T(8,128)(2,1)S(1)}, bf16[720,256]{1,0:T(8,128)(2,1)S(1)}) custom-call(s32[4,348]{1,0:T(4,128)S(1)} %bitcast.19, f32[2,6048,128]{2,1,0:T(8,128)S(1)} %get-tuple-element.14.total_ref, f32[6048,128]{1,0:T(8,128)S(1)} %get-tuple-element.15.totalw_ref), custom_call_target="tpu_custom_call" | custom-call | flops 5000000000 | bytes 20000000 | tf_op jit(solution)/shard_map/pack/pallas_call | solution.py:434
  34.6 2.5 %collective-permute-start = (bf16[720,256]{1,0:T(8,128)(2,1)S(1)}, bf16[720,256]{1,0:T(8,128)(2,1)S(1)}, u32[]{:S(2)}, u32[]{:S(2)}) collective-permute-start(bf16[720,256]{1,0:T(8,128)(2,1)S(1)} %get-tuple-element.16), channel_id=1, source_target_pairs={{0,16},{16,32},{32,48},{48,64},{64,80},{80,96},{96,112},{112,0},{1... | collective-permute-start | bytes 1105928 | tf_op jit(solution)/shard_map/ppermute | solution.py:24
  37.2 0.0 collective-permute-start.1
  37.2 0.7 %divide.1.total_ref = f32[2,6048,128]{2,1,0:T(8,128)S(1)} custom-call(f32[2,6048,128]{2,1,0:T(8,128)S(1)} %get-tuple-element.14.total_ref, f32[6048,128]{1,0:T(8,128)S(1)} %get-tuple-element.15.totalw_ref), custom_call_target="tpu_custom_call", output_to_operand_aliasing={{}: (0, {})} | custom-call | flops 2000000000 | bytes 12000000 | tf_op jit(solution)/shard_map/divide/pallas_call | solution.py:445
  37.9 2.4 %collective-permute-done.2.in2_ref = bf16[720,256]{1,0:T(8,128)(2,1)S(1)} collective-permute-done((bf16[720,256]{1,0:T(8,128)(2,1)S(1)}, bf16[720,256]{1,0:T(8,128)(2,1)S(1)}, u32[]{:S(2)}, u32[]{:S(2)}) %collective-permute-start.2) | collective-permute-done | bytes 368672 | tf_op jit(solution)/shard_map/ppermute | solution.py:24
  40.2 0.0 collective-permute-done.3.in3_ref
  40.3 2.5 %early.1.total_ref = f32[2,6048,128]{2,1,0:T(8,128)S(1)} custom-call(s32[4,348]{1,0:T(4,128)S(1)} %bitcast.20, bf16[720,256]{1,0:T(8,128)(2,1)S(1)} %collective-permute-done.2.in2_ref, bf16[720,256]{1,0:T(8,128)(2,1)S(1)} %collective-permute-done.3.in3_ref, f32[2,6048,128]{2,1,0:T(8,128)S(1)} %divide.1.total_ref, ...), custom_call_target="tpu_custom_call", output_to_operand_aliasing={{}: (3, {})} | custom-call | flops 5000000000 | bytes 20000000 | tf_op jit(solution)/shard_map/early/pallas_call | solution.py:456
  42.8 0.0 collective-permute-done.in0_ref
  42.8 1.3 %collective-permute-done.1.in1_ref = bf16[720,256]{1,0:T(8,128)(2,1)S(1)} collective-permute-done((bf16[720,256]{1,0:T(8,128)(2,1)S(1)}, bf16[720,256]{1,0:T(8,128)(2,1)S(1)}, u32[]{:S(2)}, u32[]{:S(2)}) %collective-permute-start.1) | collective-permute-done | bytes 368672 | tf_op jit(solution)/shard_map/ppermute | solution.py:24
  44.1 17.0 %recover.1 = (f32[4608,256]{1,0:T(8,128)}, bf16[125,64,256]{2,1,0:T(8,128)(2,1)}, f32[2,6048,128]{2,1,0:T(8,128)S(1)}) custom-call(s32[1,1]{1,0:T(1,128)S(6)} %copy.17.count_ref, s32[4,348]{1,0:T(4,128)S(1)} %bitcast.21, bf16[720,256]{1,0:T(8,128)(2,1)S(1)} %collective-permute-done.in0_ref, ...), custom_call_target="tpu_custom_call", output_to_operand_aliasing={{2}: (4, {})} | custom-call | tf_op jit(solution)/shard_map/recover/pallas_call | solution.py:468
Async XLA Ops:
  1.3 0.7 %copy-start = (s32[1,1,4,348]{3,2,1,0:T(4,128)S(1)}, s32[1,1,4,348]{3,2,1,0:T(4,128)}, u32[]{:S(2)}) copy-start(s32[1,1,4,348]{3,2,1,0:T(4,128)} %param.16) | copy-start | bytes 16708
  26.1 14.1 %collective-permute-start.2 = (bf16[720,256]{1,0:T(8,128)(2,1)S(1)}, bf16[720,256]{1,0:T(8,128)(2,1)S(1)}, u32[]{:S(2)}, u32[]{:S(2)}) collective-permute-start(bf16[720,256]{1,0:T(8,128)(2,1)S(1)} %get-tuple-element.18), channel_id=1, source_target_pairs={{0,1},{1,2},{2,3},{3,4},{4,5},{5,6},{6,7},{7,8},{8,9},{9,10},{10,1... | collective-permute-start | bytes 1105928 | tf_op jit(solution)/shard_map/ppermute | solution.py:24
  28.4 11.9 %collective-permute-start.3 = (bf16[720,256]{1,0:T(8,128)(2,1)S(1)}, bf16[720,256]{1,0:T(8,128)(2,1)S(1)}, u32[]{:S(2)}, u32[]{:S(2)}) collective-permute-start(bf16[720,256]{1,0:T(8,128)(2,1)S(1)} %get-tuple-element.19), channel_id=1, source_target_pairs={{0,15},{1,0},{2,1},{3,2},{4,3},{5,4},{6,5},{7,6},{8,7},{9,8},{10,9... | collective-permute-start | bytes 1105928 | tf_op jit(solution)/shard_map/ppermute | solution.py:24
  34.6 8.2 %collective-permute-start = (bf16[720,256]{1,0:T(8,128)(2,1)S(1)}, bf16[720,256]{1,0:T(8,128)(2,1)S(1)}, u32[]{:S(2)}, u32[]{:S(2)}) collective-permute-start(bf16[720,256]{1,0:T(8,128)(2,1)S(1)} %get-tuple-element.16), channel_id=1, source_target_pairs={{0,16},{16,32},{32,48},{48,64},{64,80},{80,96},{96,112},{112,0},{1... | collective-permute-start | bytes 1105928 | tf_op jit(solution)/shard_map/ppermute | solution.py:24
  37.2 6.9 %collective-permute-start.1 = (bf16[720,256]{1,0:T(8,128)(2,1)S(1)}, bf16[720,256]{1,0:T(8,128)(2,1)S(1)}, u32[]{:S(2)}, u32[]{:S(2)}) collective-permute-start(bf16[720,256]{1,0:T(8,128)(2,1)S(1)} %get-tuple-element.17), channel_id=1, source_target_pairs={{0,112},{16,0},{32,16},{48,32},{64,48},{80,64},{96,80},{112,96},{1... | collective-permute-start | bytes 1105928 | tf_op jit(solution)/shard_map/ppermute | solution.py:24

commit v4 on v3

--- a/solution.py
+++ b/solution.py
@@ -48,14 +48,30 @@
 
 def deinterleave(source, target):
     rows, slots, cols = source.shape
+    half_rows = target.shape[1] // (STEP // GS)
     for tile in range(target.shape[0]):
         first, end = tile * LANES, min((tile + 1) * LANES, cols)
-        block = source[:, :, first:end].astype(F32).reshape(rows * slots, end - first)
-        target[tile, 0 : rows * slots, 0 : end - first] = block
+        block = source[:, :, first:end].astype(F32)
+        for half in range(STEP // GS):
+            part = block[:, half * GS : (half + 1) * GS].reshape(rows * GS, end - first)
+            target[tile, half * half_rows : half * half_rows + rows * GS, 0 : end - first] = part
+
+
+def of_slot(target, slot, rows):
+    half_rows = target.shape[1] // (STEP // GS)
+    return pl.ds(slot // GS * half_rows + slot % GS, rows, stride=GS)
 
 
 def slot_rows(target, slot, rows):
-    return take(target, pl.ds(slot, rows, stride=STEP)).astype(BF16)
+    return take(target, of_slot(target, slot, rows)).astype(BF16)
+
+
+def clear_slots(target, rows):
+    half_rows = target.shape[1] // (STEP // GS)
+    size = half_rows - rows * GS
+    for half in range(STEP // GS):
+        first = half * half_rows + rows * GS
+        target[:, first : first + size, :] = jnp.zeros((target.shape[0], size, LANES), F32)
 
 
 def clear(ref, first):
@@ -92,16 +108,18 @@
     coup32,
     inv32,
     solved,
+    select,
 ):
     owned, shared, local, windows, modes, inner = sizes
     step = pl.program_id(0)
     mpad, ipad = up(modes, 16), up(inner, LANES)
-    wpad = op_ref.shape[1]
+    wpad = up(windows, 16)
 
     @pl.when(step == 0)
     def _():
-        clear(load32, inner * STEP)
+        clear_slots(load32, inner)
         coup32[...] = jnp.zeros_like(coup32)
+        select[...] = selectors()
         inv32[...] = jnp.zeros_like(inv32)
         live = lax.broadcasted_iota(jnp.int32, dof_ref.shape, 0) < count_ref[0, 0]
         dofp[...] = jnp.full(dofp.shape, -1, jnp.int32)
@@ -137,13 +155,14 @@
         totals = operator(
             dofp[at, :],
             weightp[at, :],
-            lambda e: take(coup32, pl.ds(half * GS + e, mpad, stride=STEP)),
+            lambda e: take(coup32, of_slot(coup32, half * GS + e, mpad)),
             op_ref.at[group],
+            select[...],
             mpad,
         )
         rows = pl.ds(group, wpad, stride=GS)
-        place(total_ref, rows, take(total_ref, rows) - nn(op_ref[group], solved[half]))
-        totalw_ref[rows, :] = totalw_ref[rows, :] + totals
+        place(total_ref, rows, take(total_ref, rows) - tn(op_ref[group], solved[half])[0:wpad])
+        totalw_ref[rows, :] = totalw_ref[rows, :] + totals[0:wpad]
 
     @pl.when(step == pl.num_programs(0) - 1)
     def _():
@@ -190,40 +209,46 @@
     pack(sizes, (0, 1), (pay0_ref, pay1_ref), readers_ref, total_ref, totalw_ref, picked_ref)
 
 
-def weight_columns(row):
-    high = row.astype(BF16).astype(F32)
-    middle = (row - high).astype(BF16).astype(F32)
-    low = row - high - middle
-    lines = lax.broadcasted_iota(jnp.int32, (LANES, 256), 0)
-    packed = jnp.where(lines == LANES - 3, jnp.broadcast_to(high, (LANES, 256)), 0.0)
-    packed = jnp.where(lines == LANES - 2, jnp.broadcast_to(middle, (LANES, 256)), packed)
-    packed = jnp.where(lines == LANES - 1, jnp.broadcast_to(low, (LANES, 256)), packed)
-    return jnp.transpose(packed)
-
-
-def operator(dofs, weights, coupling_of, target, mpad):
-    count = target.shape[0]
-    block = 256
-    wide = [jnp.broadcast_to(dofs[e : e + 1], (16, 256)).astype(jnp.int16) for e in range(GS)]
-    coup = [
-        (coupling_of(e) + weight_columns(weights[e : e + 1])[0:mpad]).astype(BF16) for e in range(GS)
-    ]
-    base = lax.broadcasted_iota(jnp.int32, (16, 256), 0)
-    parts = []
-    for chunk in range(0, count, block):
-        size = min(block, count - chunk)
-        ids = jnp.concatenate([(base + (chunk + i)).astype(jnp.int16) for i in range(0, size, 16)], axis=0)
-        one, none = jnp.ones((size, 256), BF16), jnp.zeros((size, 256), BF16)
-        total = jnp.zeros((size, LANES), F32)
-        for e in range(GS):
-            hit = jnp.where(ids == jnp.concatenate([wide[e]] * (size // 16), axis=0), one, none)
-            result = nn(hit[:, 0:mpad], coup[e])
-            target[chunk : chunk + size, e * LANES : (e + 1) * LANES] = result.astype(BF16)
-            total = total + result
-        lanes = lax.broadcasted_iota(jnp.int32, (size, LANES), 1)
-        total = jnp.sum(jnp.where(lanes >= LANES - 3, total, 0.0), axis=1, keepdims=True)
-        parts.append(jnp.broadcast_to(total, (size, LANES)))
-    return jnp.concatenate(parts, axis=0)
+def selectors():
+    line = lax.broadcasted_iota(jnp.int32, (LANES, GS * 256), 0)
+    place_at = lax.broadcasted_iota(jnp.int32, (LANES, GS * 256), 1)
+    slot, lane = lax.shift_right_logical(place_at, 8), lax.bitwise_and(place_at, 255)
+    kind, of = lax.shift_right_logical(line, 3), lax.bitwise_and(line, 7)
+    ids = (lane < LANES) & (kind < 2)
+    parts = (lane >= 253) & (kind == lane - 251)
+    return jnp.where((of == slot) & (ids | parts), 1.0, 0.0).astype(BF16)
+
+
+def columns_of(dofs, weights, select, mpad):
+    coarse = lax.shift_left(lax.shift_right_arithmetic(dofs, 3), 3)
+    high = weights.astype(BF16).astype(F32)
+    middle = (weights - high).astype(BF16).astype(F32)
+    lines = [coarse.astype(F32), (dofs - coarse).astype(F32), high, middle, weights - high - middle]
+    lines.append(jnp.zeros((LANES - 5 * GS, dofs.shape[1]), F32))
+    turned = jnp.transpose(jnp.concatenate(lines, axis=0)).astype(BF16)
+    return nn(turned[0:mpad], select)
+
+
+def operator(dofs, weights, coupling_of, target, select, mpad):
+    count = target.shape[1]
+    tiles = count // LANES
+    lane = lax.broadcasted_iota(jnp.int32, (16, LANES), 1)
+    ids = jnp.concatenate([(lane + tile * LANES).astype(jnp.int16) for tile in range(tiles)], axis=1)
+    ids = jnp.concatenate([ids] * (mpad // 16), axis=0)
+    one, none = jnp.ones((mpad, count), BF16), jnp.zeros((mpad, count), BF16)
+    total = jnp.zeros((8, count), F32)
+    columns = columns_of(dofs, weights, select, mpad)
+    for e in range(GS):
+        column = columns[:, e * 256 : e * 256 + LANES].astype(jnp.int32).astype(jnp.int16)
+        hit = jnp.where(jnp.concatenate([column] * tiles, axis=1) == ids, one, none)
+        coup = (coupling_of(e) + columns[:, e * 256 + LANES : (e + 1) * 256]).astype(BF16)
+        result = tn(coup, hit)
+        target[e * LANES : (e + 1) * LANES, :] = result.astype(BF16)
+        total = total + result[LANES - 8 :]
+    line = total[5:6] + total[6:7] + total[7:8]
+    return jnp.concatenate(
+        [column_of(line[:, tile * LANES : (tile + 1) * LANES]) for tile in range(tiles)], axis=0
+    )
 
 
 def divide_kernel(owned, total_ref, totalw_ref, out_ref):
@@ -302,7 +327,7 @@
     step = pl.program_id(0)
     count = count_ref[0, 0]
     ipad = up(inner, LANES)
-    wpad = op_ref.shape[1]
+    wpad = up(windows, 16)
 
     def stores():
         return [
@@ -316,29 +341,39 @@
 
     @pl.when(step == 0)
     def _():
-        clear(load32, inner * STEP)
+        clear_slots(load32, inner)
         absorb(sizes, (0, 1), (in0_ref, in1_ref), readers_ref, totalw_ref, picked_ref, values, shares)
         for copy in stores():
             copy.start()
 
-    deinterleave(load_ref, load32)
+    deinterleave(load_ref.at[:, pl.ds(pl.multiple_of(step * STEP, STEP), STEP), :], load32)
+    pulls = []
     for half in range(STEP // GS):
         group = step * (STEP // GS) + half
         window = take(values, pl.ds(group, wpad, stride=GS)).astype(BF16)
-        pulled = tn(op_ref[group], window)
+        window = jnp.concatenate([window, jnp.zeros((op_ref.shape[2] - wpad, window.shape[1]), BF16)], axis=0)
+        pulls.append(nn(op_ref[group], window))
+    for half in range(STEP // GS):
+        group = step * (STEP // GS) + half
+        pulled = pulls[half]
         for p in range(GS // 2):
             slot = half * GS + 2 * p
             loads = jnp.concatenate(
-                [take(load32, pl.ds(slot + j, ipad, stride=STEP)) for j in range(2)], axis=0
+                [take(load32, of_slot(load32, slot + j, ipad)) for j in range(2)], axis=0
             )
             reduced = (loads - pulled[2 * p * ipad : (2 * p + 2) * ipad]).astype(BF16)
             result = nn(pairs_ref[group * (GS // 2) + p], reduced)
             for j in range(2):
                 live = group * GS + 2 * p + j < count
                 part = jnp.where(live, result[j * ipad : (j + 1) * ipad], 0.0)
-                place(out32, pl.ds(slot + j, ipad, stride=STEP), part)
+                place(out32, of_slot(out32, slot + j, ipad), part)
     for tile in range(2):
-        block = out32[tile, 0 : inner * STEP, :].reshape(inner, STEP, LANES)
+        half_rows = out32.shape[1] // (STEP // GS)
+        block = [
+            out32[tile, half * half_rows : half * half_rows + inner * GS, :].reshape(inner, GS, LANES)
+            for half in range(STEP // GS)
+        ]
+        block = jnp.concatenate(block, axis=1)
         out_ref[:, :, tile * LANES : (tile + 1) * LANES] = block.astype(BF16)
 
     @pl.when(step == pl.num_programs(0) - 1)
@@ -375,7 +410,7 @@
     owner = far(owner_weight[0])
     weight = far(elem_weight[0, 0])
     dof = far(elem_dof[0, 0])
-    readers = reader_rows[0, 0]
+    readers = far(reader_rows[0, 0])
 
     modes, slots, inner = coupling.shape
     columns = load.shape[-1]
@@ -411,7 +446,7 @@
         out_specs=[near] * 7,
         out_shape=[
             pltpu.VMEM((slots // 2, 2 * ipad, 2 * ipad), BF16),
-            pltpu.VMEM((groups, wpad, GS * ipad), BF16),
+            pltpu.VMEM((groups, GS * ipad, up(windows, LANES)), BF16),
             pltpu.VMEM((2, nat, LANES), F32),
             pltpu.VMEM((nat, LANES), F32),
             pltpu.VMEM((3, 2 * wide, LANES), F32),
@@ -424,6 +459,7 @@
             pltpu.VMEM((1, mpad * STEP, LANES), F32),
             pltpu.VMEM((1, ipad * STEP, LANES), F32),
             pltpu.VMEM((STEP // GS, GS * ipad, columns), BF16),
+            pltpu.VMEM((LANES, GS * 256), BF16),
         ],
         compiler_params=pltpu.CompilerParams(vmem_limit_bytes=24 * 2**20),
         name="condense",
@@ -468,7 +504,7 @@
     face, interior, _ = pl.pallas_call(
         functools.partial(recover_kernel, sizes),
         grid=(steps,),
-        in_specs=[smem, smem] + [near] * 7 + [by_slot(inner, columns)],
+        in_specs=[smem, smem] + [near] * 8,
         out_specs=[pl.BlockSpec(memory_space=pltpu.HBM), by_slot(inner, columns), near],
         out_shape=[
             pltpu.HBM((owned, columns), F32),
@@ -484,7 +520,7 @@
         ],
         compiler_params=pltpu.CompilerParams(vmem_limit_bytes=23 * 2**20),
         name="recover",
-    )(elem_count, readers, *arrived, total, totalw, picked_x, operators, pairs, load)
+    )(elem_count, readers, *arrived, total, totalw, picked_x, operators, pairs, pltpu.with_memory_space_constraint(jnp.transpose(interior_load[0, 0], (1, 0, 2)), pltpu.VMEM))
     interior = jnp.transpose(interior, (1, 0, 2))
     return (face[None, None], interior[None, None])
 

time: 61.3 us -> 52.6 us (0.86)
  Pallas kernels: 47 us -> 39.1 us
  local copies, waits for them, and re-layouts: 0.68 us -> 0.01 us
    pallas_call x1, Pallas kernels: 17 us -> 11.3 us  [per_device(): pl.pallas_call(functools.partial(recover_kernel, sizes), grid=(steps,), i...]
    pallas_call x1, Pallas kernels: 24.2 us -> 21.7 us  [per_device(): pl.pallas_call(functools.partial(condense_kernel, sizes), grid=(steps,),...]
    unnamed x2, local copies, waits for them, and re-layouts: 0.68 us -> 0.01 us
  transfers between devices with their start and end apart: 4 -> 4, of which waited for: 2 -> 2; matrix products, arithmetic and copies ran while one was open for 0% -> 0% of each run, Pallas kernels for 9% -> 12%
where the time goes in v4:
time: 52.6 us; the launch traced here: 52.4 us
  Pallas kernels  39.1 us (74%)
  starting transfers between devices  8.46 us (16%)
  waiting for transfers between devices  3.43 us (7%)
  between operations  1.32 us (3%)
    pallas_call x1, Pallas kernels, per_device(): pl.pallas_call(functools.partial(condense_kernel, sizes), grid=(steps,),...  21.7 us
    pallas_call x1, Pallas kernels, per_device(): pl.pallas_call(functools.partial(recover_kernel, sizes), grid=(steps,), i...  11.3 us
    ppermute x4, starting transfers between devices, passed_along(): return lax.ppermute(value, axis, pairs)  8.46 us
    ppermute x4, waiting for transfers between devices, passed_along(): return lax.ppermute(value, axis, pairs)  3.43 us
    pallas_call x1, Pallas kernels, per_device(): pl.pallas_call(functools.partial(early_kernel, sizes), in_specs=[smem] +...  2.78 us
    pallas_call x1, Pallas kernels, per_device(): pl.pallas_call(functools.partial(pack_kernel, sizes), in_specs=[smem, nea...  2.67 us
  transfers between devices with their start and end apart: 4, of which 2 were waited for; matrix products, arithmetic and copies ran while one was open for 0% of the time, Pallas kernels for 12%

profile of v4, /device:TPU:1, one launch (start us, length us, event | category | flops | bytes accessed | tf_op | source)
XLA Modules:
  0.0 52.4 jit_solution(12573954088732000819)
XLA Ops:
  1.3 21.7 %condense.1 = (bf16[32,256,256]{2,1,0:T(8,128)(2,1)S(1)}, bf16[8,1024,768]{2,1,0:T(8,128)(2,1)S(1)}, f32[2,6048,128]{2,1,0:T(8,128)S(1)}, f32[6048,128]{1,0:T(8,...) custom-call(s32[1,1]{1,0:T(1,128)S(6)} %copy.17.count_ref, ...), custom_call_target="tpu_custom_call" | custom-call | tf_op jit(solution)/shard_map/condense/pallas_call | solution.py:432
  23.0 2.2 %collective-permute-start.2 = (bf16[720,256]{1,0:T(8,128)(2,1)S(1)}, bf16[720,256]{1,0:T(8,128)(2,1)S(1)}, u32[]{:S(2)}, u32[]{:S(2)}) collective-permute-start(bf16[720,256]{1,0:T(8,128)(2,1)S(1)} %get-tuple-element.18), channel_id=1, source_target_pairs={{0,1},{1,2},{2,3},{3,4},{4,5},{5,6},{6,7},{7,8},{8,9},{9,10},{10,1... | collective-permute-start | bytes 1105928 | tf_op jit(solution)/shard_map/ppermute | solution.py:24
  25.1 3.7 %collective-permute-start.3 = (bf16[720,256]{1,0:T(8,128)(2,1)S(1)}, bf16[720,256]{1,0:T(8,128)(2,1)S(1)}, u32[]{:S(2)}, u32[]{:S(2)}) collective-permute-start(bf16[720,256]{1,0:T(8,128)(2,1)S(1)} %get-tuple-element.19), channel_id=1, source_target_pairs={{0,15},{1,0},{2,1},{3,2},{4,3},{5,4},{6,5},{7,6},{8,7},{9,8},{10,9... | collective-permute-start | bytes 1105928 | tf_op jit(solution)/shard_map/ppermute | solution.py:24
  28.9 2.7 %pack.1 = (f32[3,768,128]{2,1,0:T(8,128)S(1)}, bf16[720,256]{1,0:T(8,128)(2,1)S(1)}, bf16[720,256]{1,0:T(8,128)(2,1)S(1)}) custom-call(s32[4,348]{1,0:T(4,128)} %bitcast.26, f32[2,6048,128]{2,1,0:T(8,128)S(1)} %get-tuple-element.14.total_ref, f32[6048,128]{1,0:T(8,128)S(1)} %get-tuple-element.15.totalw_ref), custom_call_target="tpu_custom_call" | custom-call | flops 5000000000 | bytes 20000000 | tf_op jit(solution)/shard_map/pack/pallas_call | solution.py:470
  31.5 2.5 %collective-permute-start = (bf16[720,256]{1,0:T(8,128)(2,1)S(1)}, bf16[720,256]{1,0:T(8,128)(2,1)S(1)}, u32[]{:S(2)}, u32[]{:S(2)}) collective-permute-start(bf16[720,256]{1,0:T(8,128)(2,1)S(1)} %get-tuple-element.16), channel_id=1, source_target_pairs={{0,16},{16,32},{32,48},{48,64},{64,80},{80,96},{96,112},{112,0},{1... | collective-permute-start | bytes 1105928 | tf_op jit(solution)/shard_map/ppermute | solution.py:24
  34.1 0.0 collective-permute-start.1
  34.1 0.7 %divide.1.total_ref = f32[2,6048,128]{2,1,0:T(8,128)S(1)} custom-call(f32[2,6048,128]{2,1,0:T(8,128)S(1)} %get-tuple-element.14.total_ref, f32[6048,128]{1,0:T(8,128)S(1)} %get-tuple-element.15.totalw_ref), custom_call_target="tpu_custom_call", output_to_operand_aliasing={{}: (0, {})} | custom-call | flops 2000000000 | bytes 12000000 | tf_op jit(solution)/shard_map/divide/pallas_call | solution.py:481
  34.8 2.2 %collective-permute-done.2.in2_ref = bf16[720,256]{1,0:T(8,128)(2,1)S(1)} collective-permute-done((bf16[720,256]{1,0:T(8,128)(2,1)S(1)}, bf16[720,256]{1,0:T(8,128)(2,1)S(1)}, u32[]{:S(2)}, u32[]{:S(2)}) %collective-permute-start.2) | collective-permute-done | bytes 368672 | tf_op jit(solution)/shard_map/ppermute | solution.py:24
  37.0 0.0 collective-permute-done.3.in3_ref
  37.0 0.0 copy-start
  37.0 2.8 %early.1.total_ref = f32[2,6048,128]{2,1,0:T(8,128)S(1)} custom-call(s32[4,348]{1,0:T(4,128)} %bitcast.27, bf16[720,256]{1,0:T(8,128)(2,1)S(1)} %collective-permute-done.2.in2_ref, bf16[720,256]{1,0:T(8,128)(2,1)S(1)} %collective-permute-done.3.in3_ref, f32[2,6048,128]{2,1,0:T(8,128)S(1)} %divide.1.total_ref, ...), custom_call_target="tpu_custom_call", output_to_operand_aliasing={{}: (3, {})} | custom-call | flops 5000000000 | bytes 20000000 | tf_op jit(solution)/shard_map/early/pallas_call | solution.py:492
  39.8 0.0 collective-permute-done.in0_ref
  39.8 1.2 %collective-permute-done.1.in1_ref = bf16[720,256]{1,0:T(8,128)(2,1)S(1)} collective-permute-done((bf16[720,256]{1,0:T(8,128)(2,1)S(1)}, bf16[720,256]{1,0:T(8,128)(2,1)S(1)}, u32[]{:S(2)}, u32[]{:S(2)}) %collective-permute-start.1) | collective-permute-done | bytes 368672 | tf_op jit(solution)/shard_map/ppermute | solution.py:24
  41.0 0.0 copy-done
  41.0 11.3 %recover.1 = (f32[4608,256]{1,0:T(8,128)}, bf16[125,64,256]{2,1,0:T(8,128)(2,1)}, f32[2,6048,128]{2,1,0:T(8,128)S(1)}) custom-call(s32[1,1]{1,0:T(1,128)S(6)} %copy.17.count_ref, s32[4,348]{1,0:T(4,128)} %bitcast.28, bf16[720,256]{1,0:T(8,128)(2,1)S(1)} %collective-permute-done.in0_ref, ...), custom_call_target="tpu_custom_call", output_to_operand_aliasing={{2}: (4, {})} | custom-call | tf_op jit(solution)/shard_map/recover/pallas_call | solution.py:504
Async XLA Ops:
  23.0 14.1 %collective-permute-start.2 = (bf16[720,256]{1,0:T(8,128)(2,1)S(1)}, bf16[720,256]{1,0:T(8,128)(2,1)S(1)}, u32[]{:S(2)}, u32[]{:S(2)}) collective-permute-start(bf16[720,256]{1,0:T(8,128)(2,1)S(1)} %get-tuple-element.18), channel_id=1, source_target_pairs={{0,1},{1,2},{2,3},{3,4},{4,5},{5,6},{6,7},{7,8},{8,9},{9,10},{10,1... | collective-permute-start | bytes 1105928 | tf_op jit(solution)/shard_map/ppermute | solution.py:24
  25.1 11.9 %collective-permute-start.3 = (bf16[720,256]{1,0:T(8,128)(2,1)S(1)}, bf16[720,256]{1,0:T(8,128)(2,1)S(1)}, u32[]{:S(2)}, u32[]{:S(2)}) collective-permute-start(bf16[720,256]{1,0:T(8,128)(2,1)S(1)} %get-tuple-element.19), channel_id=1, source_target_pairs={{0,15},{1,0},{2,1},{3,2},{4,3},{5,4},{6,5},{7,6},{8,7},{9,8},{10,9... | collective-permute-start | bytes 1105928 | tf_op jit(solution)/shard_map/ppermute | solution.py:24
  31.5 8.3 %collective-permute-start = (bf16[720,256]{1,0:T(8,128)(2,1)S(1)}, bf16[720,256]{1,0:T(8,128)(2,1)S(1)}, u32[]{:S(2)}, u32[]{:S(2)}) collective-permute-start(bf16[720,256]{1,0:T(8,128)(2,1)S(1)} %get-tuple-element.16), channel_id=1, source_target_pairs={{0,16},{16,32},{32,48},{48,64},{64,80},{80,96},{96,112},{112,0},{1... | collective-permute-start | bytes 1105928 | tf_op jit(solution)/shard_map/ppermute | solution.py:24
  34.1 6.9 %collective-permute-start.1 = (bf16[720,256]{1,0:T(8,128)(2,1)S(1)}, bf16[720,256]{1,0:T(8,128)(2,1)S(1)}, u32[]{:S(2)}, u32[]{:S(2)}) collective-permute-start(bf16[720,256]{1,0:T(8,128)(2,1)S(1)} %get-tuple-element.17), channel_id=1, source_target_pairs={{0,112},{16,0},{32,16},{48,32},{64,48},{80,64},{96,80},{112,96},{1... | collective-permute-start | bytes 1105928 | tf_op jit(solution)/shard_map/ppermute | solution.py:24
  37.0 4.0 %copy-start = (bf16[1,1,64,125,256]{4,2,3,1,0:T(8,128)(2,1)S(1)}, bf16[1,1,64,125,256]{4,2,3,1,0:T(8,128)(2,1)}, u32[]{:S(2)}) copy-start(bf16[1,1,64,125,256]{4,2,3,1,0:T(8,128)(2,1)} %param.11) | copy-start | bytes 12288004

commit v5 on v4

--- a/solution.py
+++ b/solution.py
@@ -30,6 +30,16 @@
 
 def tn(a, b):
     return lax.dot_general(a, b, (((0,), (0,)), ((), ())), preferred_element_type=F32)
+
+
+def in_batches(step, total, batch):
+    def body(i, _):
+        step(i * batch, batch)
+        return 0
+
+    lax.fori_loop(0, total // batch, body, 0)
+    if total % batch:
+        step(total // batch * batch, total % batch)
 
 
 def column_of(row):
@@ -152,6 +162,10 @@
                 [slot_rows(load32, slot, ipad), slot_rows(load32, slot + 1, ipad)], axis=0
             )
             solved[half, 2 * p * ipad : (2 * p + 2) * ipad, :] = nn(both, loads).astype(BF16)
+    sums = []
+    for half in range(STEP // GS):
+        group = step * (STEP // GS) + half
+        at = pl.ds(pl.multiple_of(group * GS, GS), GS)
         totals = operator(
             dofp[at, :],
             weightp[at, :],
@@ -160,6 +174,10 @@
             select[...],
             mpad,
         )
+        sums.append(totals)
+    for half in range(STEP // GS):
+        group = step * (STEP // GS) + half
+        totals = sums[half]
         rows = pl.ds(group, wpad, stride=GS)
         place(total_ref, rows, take(total_ref, rows) - tn(op_ref[group], solved[half])[0:wpad])
         totalw_ref[rows, :] = totalw_ref[rows, :] + totals[0:wpad]
@@ -173,22 +191,22 @@
     owned, shared, local, windows, modes, inner = sizes
     sp, wide = up(shared, 16), up(shared, LANES)
     chunks = wide // LANES
-    batch = 29
+    batch = 48
     for slot, k in enumerate(directions):
         first = slot * wide + shared
         picked_ref[0:2, first : first + wide - shared, :] = jnp.zeros((2, wide - shared, LANES), F32)
         picked_ref[2, first : first + wide - shared, :] = jnp.ones((wide - shared, LANES), F32)
 
-        def pick(i, _):
-            for j in range(batch):
-                s = i * batch + j
-                row = readers_ref[k, s]
-                picked_ref[0, pl.ds(slot * wide + s, 1), :] = total_ref[0, pl.ds(row, 1), :]
-                picked_ref[1, pl.ds(slot * wide + s, 1), :] = total_ref[1, pl.ds(row, 1), :]
-                picked_ref[2, pl.ds(slot * wide + s, 1), :] = totalw_ref[pl.ds(row, 1), :]
-            return 0
-
-        lax.fori_loop(0, shared // batch, pick, 0)
+        def pick(first, count):
+            at = pl.ds(pl.multiple_of(slot * wide + first, 8), up(count, 8))
+            near = [picked_ref.at[part, at] for part in range(3)]
+            for j in range(count):
+                row = pl.ds(readers_ref[k, first + j], 1)
+                near[0][j : j + 1, :] = total_ref[0, row, :]
+                near[1][j : j + 1, :] = total_ref[1, row, :]
+                near[2][j : j + 1, :] = totalw_ref[row, :]
+
+        in_batches(pick, shared, batch)
 
     for slot, (k, pay) in enumerate(zip(directions, pays)):
         first = owned + k * shared
@@ -283,18 +301,18 @@
             shares[tile, slot * sp : slot * sp + shared, :] = (mine + inc[0:shared, lane].astype(F32)) * inverse
             sent = values[tile, first : first + shared, :]
             values[tile, first : first + shared, :] = (inc[sp : sp + shared, lane].astype(F32) + sent) * inverse_far
-    batch = 29
+    batch = 48
     for slot, k in enumerate(directions):
 
-        def put(i, _):
-            for j in range(batch):
-                s = i * batch + j
-                row = readers_ref[k, s]
+        def put(first, count):
+            at = pl.ds(pl.multiple_of(slot * sp + first, 8), up(count, 8))
+            near = [shares.at[tile, at] for tile in range(2)]
+            for j in range(count):
+                row = pl.ds(readers_ref[k, first + j], 1)
                 for tile in range(2):
-                    values[tile, pl.ds(row, 1), :] = shares[tile, pl.ds(slot * sp + s, 1), :]
-            return 0
-
-        lax.fori_loop(0, shared // batch, put, 0)
+                    values[tile, row, :] = near[tile][j : j + 1, :]
+
+        in_batches(put, shared, batch)
 
 
 def early_kernel(
@@ -353,20 +371,19 @@
         window = take(values, pl.ds(group, wpad, stride=GS)).astype(BF16)
         window = jnp.concatenate([window, jnp.zeros((op_ref.shape[2] - wpad, window.shape[1]), BF16)], axis=0)
         pulls.append(nn(op_ref[group], window))
-    for half in range(STEP // GS):
-        group = step * (STEP // GS) + half
-        pulled = pulls[half]
-        for p in range(GS // 2):
-            slot = half * GS + 2 * p
-            loads = jnp.concatenate(
-                [take(load32, of_slot(load32, slot + j, ipad)) for j in range(2)], axis=0
-            )
-            reduced = (loads - pulled[2 * p * ipad : (2 * p + 2) * ipad]).astype(BF16)
-            result = nn(pairs_ref[group * (GS // 2) + p], reduced)
-            for j in range(2):
-                live = group * GS + 2 * p + j < count
-                part = jnp.where(live, result[j * ipad : (j + 1) * ipad], 0.0)
-                place(out32, of_slot(out32, slot + j, ipad), part)
+    reduced = []
+    for slot in range(0, STEP, 2):
+        loads = jnp.concatenate([take(load32, of_slot(load32, slot + j, ipad)) for j in range(2)], axis=0)
+        first = slot % GS * ipad
+        reduced.append((loads - pulls[slot // GS][first : first + 2 * ipad]).astype(BF16))
+    results = [
+        nn(pairs_ref[step * (STEP // 2) + slot // 2], reduced[slot // 2]) for slot in range(0, STEP, 2)
+    ]
+    for slot in range(STEP):
+        live = step * STEP + slot < count
+        first = slot % 2 * ipad
+        part = jnp.where(live, results[slot // 2][first : first + ipad], 0.0)
+        place(out32, of_slot(out32, slot, ipad), part)
     for tile in range(2):
         half_rows = out32.shape[1] // (STEP // GS)
         block = [

time: 52.6 us -> 50.2 us (0.954)
  Pallas kernels: 39.1 us -> 36.7 us
    pallas_call x1, Pallas kernels: 21.7 us -> 19.4 us  [per_device(): pl.pallas_call(functools.partial(condense_kernel, sizes), grid=(steps,),...]
where the time goes in v5:
time: 50.2 us; the launch traced here: 50 us
  Pallas kernels  36.7 us (73%)
  starting transfers between devices  8.46 us (17%)
  waiting for transfers between devices  3.51 us (7%)
  between operations  1.32 us (3%)
    pallas_call x1, Pallas kernels, per_device(): pl.pallas_call(functools.partial(condense_kernel, sizes), grid=(steps,),...  19.4 us
    pallas_call x1, Pallas kernels, per_device(): pl.pallas_call(functools.partial(recover_kernel, sizes), grid=(steps,), i...  11.2 us
    ppermute x4, starting transfers between devices, passed_along(): return lax.ppermute(value, axis, pairs)  8.46 us
    ppermute x4, waiting for transfers between devices, passed_along(): return lax.ppermute(value, axis, pairs)  3.51 us
    pallas_call x1, Pallas kernels, per_device(): pl.pallas_call(functools.partial(early_kernel, sizes), in_specs=[smem] +...  2.69 us
    pallas_call x1, Pallas kernels, per_device(): pl.pallas_call(functools.partial(pack_kernel, sizes), in_specs=[smem, nea...  2.58 us
  transfers between devices with their start and end apart: 4, of which 2 were waited for; matrix products, arithmetic and copies ran while one was open for 0% of the time, Pallas kernels for 12%

profile of v5, /device:TPU:1, one launch (start us, length us, event | category | flops | bytes accessed | tf_op | source)
XLA Modules:
  0.0 50.0 jit_solution(13214257472905657573)
XLA Ops:
  1.3 19.4 %condense.1 = (bf16[32,256,256]{2,1,0:T(8,128)(2,1)S(1)}, bf16[8,1024,768]{2,1,0:T(8,128)(2,1)S(1)}, f32[2,6048,128]{2,1,0:T(8,128)S(1)}, f32[6048,128]{1,0:T(8,...) custom-call(s32[1,1]{1,0:T(1,128)S(6)} %copy.17.count_ref, ...), custom_call_target="tpu_custom_call" | custom-call | tf_op jit(solution)/shard_map/condense/pallas_call | solution.py:449
  20.7 2.2 %collective-permute-start.2 = (bf16[720,256]{1,0:T(8,128)(2,1)S(1)}, bf16[720,256]{1,0:T(8,128)(2,1)S(1)}, u32[]{:S(2)}, u32[]{:S(2)}) collective-permute-start(bf16[720,256]{1,0:T(8,128)(2,1)S(1)} %get-tuple-element.18), channel_id=1, source_target_pairs={{0,1},{1,2},{2,3},{3,4},{4,5},{5,6},{6,7},{7,8},{8,9},{9,10},{10,1... | collective-permute-start | bytes 1105928 | tf_op jit(solution)/shard_map/ppermute | solution.py:24
  22.9 3.7 %collective-permute-start.3 = (bf16[720,256]{1,0:T(8,128)(2,1)S(1)}, bf16[720,256]{1,0:T(8,128)(2,1)S(1)}, u32[]{:S(2)}, u32[]{:S(2)}) collective-permute-start(bf16[720,256]{1,0:T(8,128)(2,1)S(1)} %get-tuple-element.19), channel_id=1, source_target_pairs={{0,15},{1,0},{2,1},{3,2},{4,3},{5,4},{6,5},{7,6},{8,7},{9,8},{10,9... | collective-permute-start | bytes 1105928 | tf_op jit(solution)/shard_map/ppermute | solution.py:24
  26.6 2.6 %pack.1 = (f32[3,768,128]{2,1,0:T(8,128)S(1)}, bf16[720,256]{1,0:T(8,128)(2,1)S(1)}, bf16[720,256]{1,0:T(8,128)(2,1)S(1)}) custom-call(s32[4,348]{1,0:T(4,128)} %bitcast.26, f32[2,6048,128]{2,1,0:T(8,128)S(1)} %get-tuple-element.14.total_ref, f32[6048,128]{1,0:T(8,128)S(1)} %get-tuple-element.15.totalw_ref), custom_call_target="tpu_custom_call" | custom-call | flops 5000000000 | bytes 20000000 | tf_op jit(solution)/shard_map/pack/pallas_call | solution.py:487
  29.2 2.5 %collective-permute-start = (bf16[720,256]{1,0:T(8,128)(2,1)S(1)}, bf16[720,256]{1,0:T(8,128)(2,1)S(1)}, u32[]{:S(2)}, u32[]{:S(2)}) collective-permute-start(bf16[720,256]{1,0:T(8,128)(2,1)S(1)} %get-tuple-element.16), channel_id=1, source_target_pairs={{0,16},{16,32},{32,48},{48,64},{64,80},{80,96},{96,112},{112,0},{1... | collective-permute-start | bytes 1105928 | tf_op jit(solution)/shard_map/ppermute | solution.py:24
  31.8 0.0 collective-permute-start.1
  31.8 0.7 %divide.1.total_ref = f32[2,6048,128]{2,1,0:T(8,128)S(1)} custom-call(f32[2,6048,128]{2,1,0:T(8,128)S(1)} %get-tuple-element.14.total_ref, f32[6048,128]{1,0:T(8,128)S(1)} %get-tuple-element.15.totalw_ref), custom_call_target="tpu_custom_call", output_to_operand_aliasing={{}: (0, {})} | custom-call | flops 2000000000 | bytes 12000000 | tf_op jit(solution)/shard_map/divide/pallas_call | solution.py:498
  32.5 2.3 %collective-permute-done.2.in2_ref = bf16[720,256]{1,0:T(8,128)(2,1)S(1)} collective-permute-done((bf16[720,256]{1,0:T(8,128)(2,1)S(1)}, bf16[720,256]{1,0:T(8,128)(2,1)S(1)}, u32[]{:S(2)}, u32[]{:S(2)}) %collective-permute-start.2) | collective-permute-done | bytes 368672 | tf_op jit(solution)/shard_map/ppermute | solution.py:24
  34.8 0.0 collective-permute-done.3.in3_ref
  34.8 0.0 copy-start
  34.8 2.7 %early.1.total_ref = f32[2,6048,128]{2,1,0:T(8,128)S(1)} custom-call(s32[4,348]{1,0:T(4,128)} %bitcast.27, bf16[720,256]{1,0:T(8,128)(2,1)S(1)} %collective-permute-done.2.in2_ref, bf16[720,256]{1,0:T(8,128)(2,1)S(1)} %collective-permute-done.3.in3_ref, f32[2,6048,128]{2,1,0:T(8,128)S(1)} %divide.1.total_ref, ...), custom_call_target="tpu_custom_call", output_to_operand_aliasing={{}: (3, {})} | custom-call | flops 5000000000 | bytes 20000000 | tf_op jit(solution)/shard_map/early/pallas_call | solution.py:509
  37.5 0.0 collective-permute-done.in0_ref
  37.5 1.2 %collective-permute-done.1.in1_ref = bf16[720,256]{1,0:T(8,128)(2,1)S(1)} collective-permute-done((bf16[720,256]{1,0:T(8,128)(2,1)S(1)}, bf16[720,256]{1,0:T(8,128)(2,1)S(1)}, u32[]{:S(2)}, u32[]{:S(2)}) %collective-permute-start.1) | collective-permute-done | bytes 368672 | tf_op jit(solution)/shard_map/ppermute | solution.py:24
  38.7 0.0 copy-done
  38.7 11.2 %recover.1 = (f32[4608,256]{1,0:T(8,128)}, bf16[125,64,256]{2,1,0:T(8,128)(2,1)}, f32[2,6048,128]{2,1,0:T(8,128)S(1)}) custom-call(s32[1,1]{1,0:T(1,128)S(6)} %copy.17.count_ref, s32[4,348]{1,0:T(4,128)} %bitcast.28, bf16[720,256]{1,0:T(8,128)(2,1)S(1)} %collective-permute-done.in0_ref, ...), custom_call_target="tpu_custom_call", output_to_operand_aliasing={{2}: (4, {})} | custom-call | tf_op jit(solution)/shard_map/recover/pallas_call | solution.py:521
Async XLA Ops:
  20.7 14.1 %collective-permute-start.2 = (bf16[720,256]{1,0:T(8,128)(2,1)S(1)}, bf16[720,256]{1,0:T(8,128)(2,1)S(1)}, u32[]{:S(2)}, u32[]{:S(2)}) collective-permute-start(bf16[720,256]{1,0:T(8,128)(2,1)S(1)} %get-tuple-element.18), channel_id=1, source_target_pairs={{0,1},{1,2},{2,3},{3,4},{4,5},{5,6},{6,7},{7,8},{8,9},{9,10},{10,1... | collective-permute-start | bytes 1105928 | tf_op jit(solution)/shard_map/ppermute | solution.py:24
  22.9 11.9 %collective-permute-start.3 = (bf16[720,256]{1,0:T(8,128)(2,1)S(1)}, bf16[720,256]{1,0:T(8,128)(2,1)S(1)}, u32[]{:S(2)}, u32[]{:S(2)}) collective-permute-start(bf16[720,256]{1,0:T(8,128)(2,1)S(1)} %get-tuple-element.19), channel_id=1, source_target_pairs={{0,15},{1,0},{2,1},{3,2},{4,3},{5,4},{6,5},{7,6},{8,7},{9,8},{10,9... | collective-permute-start | bytes 1105928 | tf_op jit(solution)/shard_map/ppermute | solution.py:24
  29.2 8.3 %collective-permute-start = (bf16[720,256]{1,0:T(8,128)(2,1)S(1)}, bf16[720,256]{1,0:T(8,128)(2,1)S(1)}, u32[]{:S(2)}, u32[]{:S(2)}) collective-permute-start(bf16[720,256]{1,0:T(8,128)(2,1)S(1)} %get-tuple-element.16), channel_id=1, source_target_pairs={{0,16},{16,32},{32,48},{48,64},{64,80},{80,96},{96,112},{112,0},{1... | collective-permute-start | bytes 1105928 | tf_op jit(solution)/shard_map/ppermute | solution.py:24
  31.8 6.9 %collective-permute-start.1 = (bf16[720,256]{1,0:T(8,128)(2,1)S(1)}, bf16[720,256]{1,0:T(8,128)(2,1)S(1)}, u32[]{:S(2)}, u32[]{:S(2)}) collective-permute-start(bf16[720,256]{1,0:T(8,128)(2,1)S(1)} %get-tuple-element.17), channel_id=1, source_target_pairs={{0,112},{16,0},{32,16},{48,32},{64,48},{80,64},{96,80},{112,96},{1... | collective-permute-start | bytes 1105928 | tf_op jit(solution)/shard_map/ppermute | solution.py:24
  34.8 3.9 %copy-start = (bf16[1,1,64,125,256]{4,2,3,1,0:T(8,128)(2,1)S(1)}, bf16[1,1,64,125,256]{4,2,3,1,0:T(8,128)(2,1)}, u32[]{:S(2)}) copy-start(bf16[1,1,64,125,256]{4,2,3,1,0:T(8,128)(2,1)} %param.11) | copy-start | bytes 12288004

commit v6 on v5

--- a/solution.py
+++ b/solution.py
@@ -175,11 +175,12 @@
             mpad,
         )
         sums.append(totals)
+    added = [tn(op_ref[step * (STEP // GS) + half], solved[half])[0:wpad] for half in range(STEP // GS)]
     for half in range(STEP // GS):
         group = step * (STEP // GS) + half
         totals = sums[half]
         rows = pl.ds(group, wpad, stride=GS)
-        place(total_ref, rows, take(total_ref, rows) - tn(op_ref[group], solved[half])[0:wpad])
+        place(total_ref, rows, take(total_ref, rows) - added[half])
         totalw_ref[rows, :] = totalw_ref[rows, :] + totals[0:wpad]
 
     @pl.when(step == pl.num_programs(0) - 1)
@@ -292,12 +293,12 @@
         sums = sums[:, 0:LANES] + sums[:, LANES:]
         columns = [column_of(sums[c : c + 1]) for c in range(2 * chunks)]
         theirs = jnp.concatenate(columns[:chunks], axis=0)[0:shared]
-        inverse = 1.0 / (picked_ref[2, slot * wide : slot * wide + shared, :] + theirs)
+        inverse = 1.0 / (picked_ref[2, k % 2 * wide : k % 2 * wide + shared, :] + theirs)
         far = jnp.concatenate(columns[chunks:], axis=0)[0:shared]
         inverse_far = 1.0 / (far + totalw_ref[first : first + shared, :])
         for tile in range(2):
             lane = slice(tile * LANES, (tile + 1) * LANES)
-            mine = picked_ref[tile, slot * wide : slot * wide + shared, :]
+            mine = picked_ref[tile, k % 2 * wide : k % 2 * wide + shared, :]
             shares[tile, slot * sp : slot * sp + shared, :] = (mine + inc[0:shared, lane].astype(F32)) * inverse
             sent = values[tile, first : first + shared, :]
             values[tile, first : first + shared, :] = (inc[sp : sp + shared, lane].astype(F32) + sent) * inverse_far
@@ -316,9 +317,9 @@
 
 
 def early_kernel(
-    sizes, readers_ref, in2_ref, in3_ref, total_ref, totalw_ref, picked_ref, values, shares
+    sizes, direction, readers_ref, in_ref, total_ref, totalw_ref, picked_ref, values, shares
 ):
-    absorb(sizes, (2, 3), (in2_ref, in3_ref), readers_ref, totalw_ref, picked_ref, values, shares)
+    absorb(sizes, (direction,), (in_ref,), readers_ref, totalw_ref, picked_ref, values, shares)
 
 
 def recover_kernel(
@@ -506,17 +507,18 @@
         name="divide",
     )(total, totalw)
 
-    total = pl.pallas_call(
-        functools.partial(early_kernel, sizes),
-        in_specs=[smem] + [near] * 5,
-        out_specs=near,
-        out_shape=pltpu.VMEM((2, nat, LANES), F32),
-        input_output_aliases={3: 0},
-        scratch_shapes=[pltpu.VMEM((2, 2 * sp, LANES), F32)],
-        cost_estimate=pl.CostEstimate(flops=5_000_000_000, bytes_accessed=20_000_000, transcendentals=0),
-        compiler_params=pltpu.CompilerParams(vmem_limit_bytes=8 * 2**20),
-        name="early",
-    )(readers, *returned, total, totalw, picked)
+    for direction, block in zip((2, 3), returned):
+        total = pl.pallas_call(
+            functools.partial(early_kernel, sizes, direction),
+            in_specs=[smem] + [near] * 4,
+            out_specs=near,
+            out_shape=pltpu.VMEM((2, nat, LANES), F32),
+            input_output_aliases={2: 0},
+            scratch_shapes=[pltpu.VMEM((2, sp, LANES), F32)],
+            cost_estimate=pl.CostEstimate(flops=2_500_000_000, bytes_accessed=10_000_000, transcendentals=0),
+            compiler_params=pltpu.CompilerParams(vmem_limit_bytes=8 * 2**20),
+            name="early",
+        )(readers, block, total, totalw, picked)
 
     face, interior, _ = pl.pallas_call(
         functools.partial(recover_kernel, sizes),

time: 50.2 us -> 54.8 us (1.092)
  waiting for transfers between devices: 3.51 us -> 6.66 us
  Pallas kernels: 36.7 us -> 37.5 us
    ppermute x4, waiting for transfers between devices: 3.51 us -> 6.66 us  [passed_along(): return lax.ppermute(value, axis, pairs)]
    pallas_call x1 -> x2, Pallas kernels: 2.69 us -> 3.51 us  [per_device(): pl.pallas_call(functools.partial(early_kernel, sizes, direction), in_spec...]
  transfers between devices with their start and end apart: 4 -> 4, of which waited for: 2 -> 1; matrix products, arithmetic and copies ran while one was open for 0% -> 0% of each run, Pallas kernels for 12% -> 13%
where the time goes in v6:
time: 54.8 us; the launch traced here: 54.1 us
  Pallas kernels  37.5 us (68%)
  starting transfers between devices  8.32 us (15%)
  waiting for transfers between devices  6.66 us (12%)
  between operations  1.35 us (2%)
    pallas_call x1, Pallas kernels, per_device(): pl.pallas_call(functools.partial(condense_kernel, sizes), grid=(steps,),...  19.5 us
    pallas_call x1, Pallas kernels, per_device(): pl.pallas_call(functools.partial(recover_kernel, sizes), grid=(steps,), i...  11.2 us
    ppermute x4, starting transfers between devices, passed_along(): return lax.ppermute(value, axis, pairs)  8.32 us
    ppermute x4, waiting for transfers between devices, passed_along(): return lax.ppermute(value, axis, pairs)  6.66 us
    pallas_call x2, Pallas kernels, per_device(): pl.pallas_call(functools.partial(early_kernel, sizes, direction), in_spec...  3.51 us
    pallas_call x1, Pallas kernels, per_device(): pl.pallas_call(functools.partial(pack_kernel, sizes), in_specs=[smem, nea...  2.58 us
  transfers between devices with their start and end apart: 4, of which 1 were waited for; matrix products, arithmetic and copies ran while one was open for 0% of the time, Pallas kernels for 13%

profile of v6, /device:TPU:1, one launch (start us, length us, event | category | flops | bytes accessed | tf_op | source)
XLA Modules:
  0.0 54.1 jit_solution(3220464329726709830)
XLA Ops:
  1.3 19.5 %condense.1 = (bf16[32,256,256]{2,1,0:T(8,128)(2,1)S(1)}, bf16[8,1024,768]{2,1,0:T(8,128)(2,1)S(1)}, f32[2,6048,128]{2,1,0:T(8,128)S(1)}, f32[6048,128]{1,0:T(8,...) custom-call(s32[1,1]{1,0:T(1,128)S(6)} %copy.19.count_ref, ...), custom_call_target="tpu_custom_call" | custom-call | tf_op jit(solution)/shard_map/condense/pallas_call | solution.py:450
  20.7 5.8 %collective-permute-start.2 = (bf16[720,256]{1,0:T(8,128)(2,1)S(1)}, bf16[720,256]{1,0:T(8,128)(2,1)S(1)}, u32[]{:S(2)}, u32[]{:S(2)}) collective-permute-start(bf16[720,256]{1,0:T(8,128)(2,1)S(1)} %get-tuple-element.18), channel_id=1, source_target_pairs={{0,15},{1,0},{2,1},{3,2},{4,3},{5,4},{6,5},{7,6},{8,7},{9,8},{10,9... | collective-permute-start | bytes 1105928 | tf_op jit(solution)/shard_map/ppermute | solution.py:24
  26.6 0.0 collective-permute-start.3
  26.6 2.6 %pack.1 = (f32[3,768,128]{2,1,0:T(8,128)S(1)}, bf16[720,256]{1,0:T(8,128)(2,1)S(1)}, bf16[720,256]{1,0:T(8,128)(2,1)S(1)}) custom-call(s32[4,348]{1,0:T(4,128)} %bitcast.24, f32[2,6048,128]{2,1,0:T(8,128)S(1)} %get-tuple-element.14.total_ref, f32[6048,128]{1,0:T(8,128)S(1)} %get-tuple-element.15.totalw_ref), custom_call_target="tpu_custom_call" | custom-call | flops 5000000000 | bytes 20000000 | tf_op jit(solution)/shard_map/pack/pallas_call | solution.py:488
  29.2 2.5 %collective-permute-start = (bf16[720,256]{1,0:T(8,128)(2,1)S(1)}, bf16[720,256]{1,0:T(8,128)(2,1)S(1)}, u32[]{:S(2)}, u32[]{:S(2)}) collective-permute-start(bf16[720,256]{1,0:T(8,128)(2,1)S(1)} %get-tuple-element.16), channel_id=1, source_target_pairs={{0,16},{16,32},{32,48},{48,64},{64,80},{80,96},{96,112},{112,0},{1... | collective-permute-start | bytes 1105928 | tf_op jit(solution)/shard_map/ppermute | solution.py:24
  31.6 0.0 collective-permute-start.1
  31.7 0.7 %divide.1.total_ref = f32[2,6048,128]{2,1,0:T(8,128)S(1)} custom-call(f32[2,6048,128]{2,1,0:T(8,128)S(1)} %get-tuple-element.14.total_ref, f32[6048,128]{1,0:T(8,128)S(1)} %get-tuple-element.15.totalw_ref), custom_call_target="tpu_custom_call", output_to_operand_aliasing={{}: (0, {})} | custom-call | flops 2000000000 | bytes 12000000 | tf_op jit(solution)/shard_map/divide/pallas_call | solution.py:499
  32.4 6.7 %collective-permute-done.3.in_ref = bf16[720,256]{1,0:T(8,128)(2,1)S(1)} collective-permute-done((bf16[720,256]{1,0:T(8,128)(2,1)S(1)}, bf16[720,256]{1,0:T(8,128)(2,1)S(1)}, u32[]{:S(2)}, u32[]{:S(2)}) %collective-permute-start.3) | collective-permute-done | bytes 368672 | tf_op jit(solution)/shard_map/ppermute | solution.py:24
  39.0 1.7 %early.2.total_ref = f32[2,6048,128]{2,1,0:T(8,128)S(1)} custom-call(s32[4,348]{1,0:T(4,128)} %bitcast.25, bf16[720,256]{1,0:T(8,128)(2,1)S(1)} %collective-permute-done.3.in_ref, f32[2,6048,128]{2,1,0:T(8,128)S(1)} %divide.1.total_ref, f32[6048,128]{1,0:T(8,128)S(1)} %get-tuple-element.15.totalw_ref, ...), custom_call_target="tpu_custom_call", output_to_operand_aliasing={{}: (2, {})} | custom-call | flops 2500000000 | bytes 10000000 | tf_op jit(solution)/shard_map/early/pallas_call | solution.py:511
  40.7 0.0 copy-start
  40.7 0.0 collective-permute-done.2.in_ref
  40.7 1.8 %early.3.total_ref = f32[2,6048,128]{2,1,0:T(8,128)S(1)} custom-call(s32[4,348]{1,0:T(4,128)} %bitcast.26, bf16[720,256]{1,0:T(8,128)(2,1)S(1)} %collective-permute-done.2.in_ref, f32[2,6048,128]{2,1,0:T(8,128)S(1)} %early.2.total_ref, f32[6048,128]{1,0:T(8,128)S(1)} %get-tuple-element.15.totalw_ref, ...), custom_call_target="tpu_custom_call", output_to_operand_aliasing={{}: (2, {})} | custom-call | flops 2500000000 | bytes 10000000 | tf_op jit(solution)/shard_map/early/pallas_call | solution.py:511
  42.6 0.0 collective-permute-done.in0_ref
  42.6 0.0 collective-permute-done.1.in1_ref
  42.6 0.3 copy-done
  42.9 11.2 %recover.1 = (f32[4608,256]{1,0:T(8,128)}, bf16[125,64,256]{2,1,0:T(8,128)(2,1)}, f32[2,6048,128]{2,1,0:T(8,128)S(1)}) custom-call(s32[1,1]{1,0:T(1,128)S(6)} %copy.19.count_ref, s32[4,348]{1,0:T(4,128)} %bitcast.27, bf16[720,256]{1,0:T(8,128)(2,1)S(1)} %collective-permute-done.in0_ref, ...), custom_call_target="tpu_custom_call", output_to_operand_aliasing={{2}: (4, {})} | custom-call | tf_op jit(solution)/shard_map/recover/pallas_call | solution.py:523
Async XLA Ops:
  20.7 20.0 %collective-permute-start.2 = (bf16[720,256]{1,0:T(8,128)(2,1)S(1)}, bf16[720,256]{1,0:T(8,128)(2,1)S(1)}, u32[]{:S(2)}, u32[]{:S(2)}) collective-permute-start(bf16[720,256]{1,0:T(8,128)(2,1)S(1)} %get-tuple-element.18), channel_id=1, source_target_pairs={{0,15},{1,0},{2,1},{3,2},{4,3},{5,4},{6,5},{7,6},{8,7},{9,8},{10,9... | collective-permute-start | bytes 1105928 | tf_op jit(solution)/shard_map/ppermute | solution.py:24
  26.6 12.5 %collective-permute-start.3 = (bf16[720,256]{1,0:T(8,128)(2,1)S(1)}, bf16[720,256]{1,0:T(8,128)(2,1)S(1)}, u32[]{:S(2)}, u32[]{:S(2)}) collective-permute-start(bf16[720,256]{1,0:T(8,128)(2,1)S(1)} %get-tuple-element.19), channel_id=1, source_target_pairs={{0,1},{1,2},{2,3},{3,4},{4,5},{5,6},{6,7},{7,8},{8,9},{9,10},{10,1... | collective-permute-start | bytes 1105928 | tf_op jit(solution)/shard_map/ppermute | solution.py:24
  29.2 13.4 %collective-permute-start = (bf16[720,256]{1,0:T(8,128)(2,1)S(1)}, bf16[720,256]{1,0:T(8,128)(2,1)S(1)}, u32[]{:S(2)}, u32[]{:S(2)}) collective-permute-start(bf16[720,256]{1,0:T(8,128)(2,1)S(1)} %get-tuple-element.16), channel_id=1, source_target_pairs={{0,16},{16,32},{32,48},{48,64},{64,80},{80,96},{96,112},{112,0},{1... | collective-permute-start | bytes 1105928 | tf_op jit(solution)/shard_map/ppermute | solution.py:24
  31.6 10.9 %collective-permute-start.1 = (bf16[720,256]{1,0:T(8,128)(2,1)S(1)}, bf16[720,256]{1,0:T(8,128)(2,1)S(1)}, u32[]{:S(2)}, u32[]{:S(2)}) collective-permute-start(bf16[720,256]{1,0:T(8,128)(2,1)S(1)} %get-tuple-element.17), channel_id=1, source_target_pairs={{0,112},{16,0},{32,16},{48,32},{64,48},{80,64},{96,80},{112,96},{1... | collective-permute-start | bytes 1105928 | tf_op jit(solution)/shard_map/ppermute | solution.py:24
  40.7 2.2 %copy-start = (bf16[1,1,64,125,256]{4,2,3,1,0:T(8,128)(2,1)S(1)}, bf16[1,1,64,125,256]{4,2,3,1,0:T(8,128)(2,1)}, u32[]{:S(2)}) copy-start(bf16[1,1,64,125,256]{4,2,3,1,0:T(8,128)(2,1)} %param.11) | copy-start | bytes 12288004

commit v7 on v5

--- a/solution.py
+++ b/solution.py
@@ -175,11 +175,12 @@
             mpad,
         )
         sums.append(totals)
+    added = [tn(op_ref[step * (STEP // GS) + half], solved[half])[0:wpad] for half in range(STEP // GS)]
     for half in range(STEP // GS):
         group = step * (STEP // GS) + half
         totals = sums[half]
         rows = pl.ds(group, wpad, stride=GS)
-        place(total_ref, rows, take(total_ref, rows) - tn(op_ref[group], solved[half])[0:wpad])
+        place(total_ref, rows, take(total_ref, rows) - added[half])
         totalw_ref[rows, :] = totalw_ref[rows, :] + totals[0:wpad]
 
     @pl.when(step == pl.num_programs(0) - 1)

time: 50.2 us -> 50.2 us (level)
  no operation moved by 1% of the time
where the time goes in v7:
time: 50.2 us; the launch traced here: 50 us
  Pallas kernels  36.7 us (73%)
  starting transfers between devices  8.46 us (17%)
  waiting for transfers between devices  3.51 us (7%)
  between operations  1.32 us (3%)
    pallas_call x1, Pallas kernels, per_device(): pl.pallas_call(functools.partial(condense_kernel, sizes), grid=(steps,),...  19.4 us
    pallas_call x1, Pallas kernels, per_device(): pl.pallas_call(functools.partial(recover_kernel, sizes), grid=(steps,), i...  11.2 us
    ppermute x4, starting transfers between devices, passed_along(): return lax.ppermute(value, axis, pairs)  8.46 us
    ppermute x4, waiting for transfers between devices, passed_along(): return lax.ppermute(value, axis, pairs)  3.51 us
    pallas_call x1, Pallas kernels, per_device(): pl.pallas_call(functools.partial(early_kernel, sizes), in_specs=[smem] +...  2.69 us
    pallas_call x1, Pallas kernels, per_device(): pl.pallas_call(functools.partial(pack_kernel, sizes), in_specs=[smem, nea...  2.59 us
  transfers between devices with their start and end apart: 4, of which 2 were waited for; matrix products, arithmetic and copies ran while one was open for 0% of the time, Pallas kernels for 12%

profile of v7, /device:TPU:1, one launch (start us, length us, event | category | flops | bytes accessed | tf_op | source)
XLA Modules:
  0.0 50.0 jit_solution(6218757378636707078)
XLA Ops:
  1.3 19.4 %condense.1 = (bf16[32,256,256]{2,1,0:T(8,128)(2,1)S(1)}, bf16[8,1024,768]{2,1,0:T(8,128)(2,1)S(1)}, f32[2,6048,128]{2,1,0:T(8,128)S(1)}, f32[6048,128]{1,0:T(8,...) custom-call(s32[1,1]{1,0:T(1,128)S(6)} %copy.17.count_ref, ...), custom_call_target="tpu_custom_call" | custom-call | tf_op jit(solution)/shard_map/condense/pallas_call | solution.py:450
  20.7 2.2 %collective-permute-start.2 = (bf16[720,256]{1,0:T(8,128)(2,1)S(1)}, bf16[720,256]{1,0:T(8,128)(2,1)S(1)}, u32[]{:S(2)}, u32[]{:S(2)}) collective-permute-start(bf16[720,256]{1,0:T(8,128)(2,1)S(1)} %get-tuple-element.18), channel_id=1, source_target_pairs={{0,1},{1,2},{2,3},{3,4},{4,5},{5,6},{6,7},{7,8},{8,9},{9,10},{10,1... | collective-permute-start | bytes 1105928 | tf_op jit(solution)/shard_map/ppermute | solution.py:24
  22.9 3.7 %collective-permute-start.3 = (bf16[720,256]{1,0:T(8,128)(2,1)S(1)}, bf16[720,256]{1,0:T(8,128)(2,1)S(1)}, u32[]{:S(2)}, u32[]{:S(2)}) collective-permute-start(bf16[720,256]{1,0:T(8,128)(2,1)S(1)} %get-tuple-element.19), channel_id=1, source_target_pairs={{0,15},{1,0},{2,1},{3,2},{4,3},{5,4},{6,5},{7,6},{8,7},{9,8},{10,9... | collective-permute-start | bytes 1105928 | tf_op jit(solution)/shard_map/ppermute | solution.py:24
  26.6 2.6 %pack.1 = (f32[3,768,128]{2,1,0:T(8,128)S(1)}, bf16[720,256]{1,0:T(8,128)(2,1)S(1)}, bf16[720,256]{1,0:T(8,128)(2,1)S(1)}) custom-call(s32[4,348]{1,0:T(4,128)} %bitcast.26, f32[2,6048,128]{2,1,0:T(8,128)S(1)} %get-tuple-element.14.total_ref, f32[6048,128]{1,0:T(8,128)S(1)} %get-tuple-element.15.totalw_ref), custom_call_target="tpu_custom_call" | custom-call | flops 5000000000 | bytes 20000000 | tf_op jit(solution)/shard_map/pack/pallas_call | solution.py:488
  29.2 2.5 %collective-permute-start = (bf16[720,256]{1,0:T(8,128)(2,1)S(1)}, bf16[720,256]{1,0:T(8,128)(2,1)S(1)}, u32[]{:S(2)}, u32[]{:S(2)}) collective-permute-start(bf16[720,256]{1,0:T(8,128)(2,1)S(1)} %get-tuple-element.16), channel_id=1, source_target_pairs={{0,16},{16,32},{32,48},{48,64},{64,80},{80,96},{96,112},{112,0},{1... | collective-permute-start | bytes 1105928 | tf_op jit(solution)/shard_map/ppermute | solution.py:24
  31.8 0.0 collective-permute-start.1
  31.8 0.7 %divide.1.total_ref = f32[2,6048,128]{2,1,0:T(8,128)S(1)} custom-call(f32[2,6048,128]{2,1,0:T(8,128)S(1)} %get-tuple-element.14.total_ref, f32[6048,128]{1,0:T(8,128)S(1)} %get-tuple-element.15.totalw_ref), custom_call_target="tpu_custom_call", output_to_operand_aliasing={{}: (0, {})} | custom-call | flops 2000000000 | bytes 12000000 | tf_op jit(solution)/shard_map/divide/pallas_call | solution.py:499
  32.5 2.3 %collective-permute-done.2.in2_ref = bf16[720,256]{1,0:T(8,128)(2,1)S(1)} collective-permute-done((bf16[720,256]{1,0:T(8,128)(2,1)S(1)}, bf16[720,256]{1,0:T(8,128)(2,1)S(1)}, u32[]{:S(2)}, u32[]{:S(2)}) %collective-permute-start.2) | collective-permute-done | bytes 368672 | tf_op jit(solution)/shard_map/ppermute | solution.py:24
  34.8 0.0 collective-permute-done.3.in3_ref
  34.8 0.0 copy-start
  34.8 2.7 %early.1.total_ref = f32[2,6048,128]{2,1,0:T(8,128)S(1)} custom-call(s32[4,348]{1,0:T(4,128)} %bitcast.27, bf16[720,256]{1,0:T(8,128)(2,1)S(1)} %collective-permute-done.2.in2_ref, bf16[720,256]{1,0:T(8,128)(2,1)S(1)} %collective-permute-done.3.in3_ref, f32[2,6048,128]{2,1,0:T(8,128)S(1)} %divide.1.total_ref, ...), custom_call_target="tpu_custom_call", output_to_operand_aliasing={{}: (3, {})} | custom-call | flops 5000000000 | bytes 20000000 | tf_op jit(solution)/shard_map/early/pallas_call | solution.py:510
  37.5 0.0 collective-permute-done.in0_ref
  37.5 1.2 %collective-permute-done.1.in1_ref = bf16[720,256]{1,0:T(8,128)(2,1)S(1)} collective-permute-done((bf16[720,256]{1,0:T(8,128)(2,1)S(1)}, bf16[720,256]{1,0:T(8,128)(2,1)S(1)}, u32[]{:S(2)}, u32[]{:S(2)}) %collective-permute-start.1) | collective-permute-done | bytes 368672 | tf_op jit(solution)/shard_map/ppermute | solution.py:24
  38.7 0.0 copy-done
  38.7 11.2 %recover.1 = (f32[4608,256]{1,0:T(8,128)}, bf16[125,64,256]{2,1,0:T(8,128)(2,1)}, f32[2,6048,128]{2,1,0:T(8,128)S(1)}) custom-call(s32[1,1]{1,0:T(1,128)S(6)} %copy.17.count_ref, s32[4,348]{1,0:T(4,128)} %bitcast.28, bf16[720,256]{1,0:T(8,128)(2,1)S(1)} %collective-permute-done.in0_ref, ...), custom_call_target="tpu_custom_call", output_to_operand_aliasing={{2}: (4, {})} | custom-call | tf_op jit(solution)/shard_map/recover/pallas_call | solution.py:522
Async XLA Ops:
  20.7 14.1 %collective-permute-start.2 = (bf16[720,256]{1,0:T(8,128)(2,1)S(1)}, bf16[720,256]{1,0:T(8,128)(2,1)S(1)}, u32[]{:S(2)}, u32[]{:S(2)}) collective-permute-start(bf16[720,256]{1,0:T(8,128)(2,1)S(1)} %get-tuple-element.18), channel_id=1, source_target_pairs={{0,1},{1,2},{2,3},{3,4},{4,5},{5,6},{6,7},{7,8},{8,9},{9,10},{10,1... | collective-permute-start | bytes 1105928 | tf_op jit(solution)/shard_map/ppermute | solution.py:24
  22.9 11.9 %collective-permute-start.3 = (bf16[720,256]{1,0:T(8,128)(2,1)S(1)}, bf16[720,256]{1,0:T(8,128)(2,1)S(1)}, u32[]{:S(2)}, u32[]{:S(2)}) collective-permute-start(bf16[720,256]{1,0:T(8,128)(2,1)S(1)} %get-tuple-element.19), channel_id=1, source_target_pairs={{0,15},{1,0},{2,1},{3,2},{4,3},{5,4},{6,5},{7,6},{8,7},{9,8},{10,9... | collective-permute-start | bytes 1105928 | tf_op jit(solution)/shard_map/ppermute | solution.py:24
  29.2 8.3 %collective-permute-start = (bf16[720,256]{1,0:T(8,128)(2,1)S(1)}, bf16[720,256]{1,0:T(8,128)(2,1)S(1)}, u32[]{:S(2)}, u32[]{:S(2)}) collective-permute-start(bf16[720,256]{1,0:T(8,128)(2,1)S(1)} %get-tuple-element.16), channel_id=1, source_target_pairs={{0,16},{16,32},{32,48},{48,64},{64,80},{80,96},{96,112},{112,0},{1... | collective-permute-start | bytes 1105928 | tf_op jit(solution)/shard_map/ppermute | solution.py:24
  31.8 6.9 %collective-permute-start.1 = (bf16[720,256]{1,0:T(8,128)(2,1)S(1)}, bf16[720,256]{1,0:T(8,128)(2,1)S(1)}, u32[]{:S(2)}, u32[]{:S(2)}) collective-permute-start(bf16[720,256]{1,0:T(8,128)(2,1)S(1)} %get-tuple-element.17), channel_id=1, source_target_pairs={{0,112},{16,0},{32,16},{48,32},{64,48},{80,64},{96,80},{112,96},{1... | collective-permute-start | bytes 1105928 | tf_op jit(solution)/shard_map/ppermute | solution.py:24
  34.8 3.9 %copy-start = (bf16[1,1,64,125,256]{4,2,3,1,0:T(8,128)(2,1)S(1)}, bf16[1,1,64,125,256]{4,2,3,1,0:T(8,128)(2,1)}, u32[]{:S(2)}) copy-start(bf16[1,1,64,125,256]{4,2,3,1,0:T(8,128)(2,1)} %param.11) | copy-start | bytes 12288004
